TPU v7x, 32 devices: a whole 2x2x4 slice. The times are simulated.
32 devices in a mesh: elem: 8 (over y, x, core), band: 4 (over z).
Axes of the slice: x: 2, y: 2, z: 4, core: 2. Of those that a mesh axis runs over, the one named last changes fastest.
Arguments:
- orbitals: bfloat16 [8, 512, 13824], P('elem', 'band'), may hold values from -6 to 6
- potential: float32 [8, 13824], P('elem'), may hold values from 0 to 1.9
- basis_count: int32 [8], P('elem'), may hold values from 256 to 512, as said below
- states: bfloat16 [8, 512, 512], P('elem', None, 'band'), may hold values from -6 to 6
Outputs:
- filtered_states: bfloat16 [8, 512, 512], P('elem', None, 'band')
Inputs may be any that keep to these rules, and one draw needn't show every extreme that they name: `basis_count`: some element keeps all 512 basis functions and some element keeps 512 // 2 of them in every draw.
All inputs are finite; a program needn't handle non-finite values.
Results may differ from a plain program's by a relative error of at most 0.03.
Values may be sent and summed in bfloat16 or wider, within the bound.
A program may use at most 64 MiB of HBM per device.

v0:
```python
import jax
import jax.numpy as jnp
from jax import lax
from jax.sharding import PartitionSpec as P

P_SIZE = 24
G = 13824
EB = 4


LOW_EDGE = 4.0
HIGH_EDGE = 14.0
PENALTY = 1.0
SHIFT_CENTER = 4.0
HALF_WIDTH = 6.0
HIGHEST = lax.Precision.HIGHEST


def with_halo(value, sides, width):
    for axis, dim in sides:
        devices, length = (lax.axis_size(axis), value.shape[dim])
        up = [(i, (i + 1) % devices) for i in range(devices - 1)]
        down = [(j, i) for i, j in up]
        last = lax.slice_in_dim(value, length - width, length, axis=dim)
        initial = lax.slice_in_dim(value, 0, width, axis=dim)
        before = lax.ppermute(last, axis, up)
        after = lax.ppermute(initial, axis, down)
        value = jnp.concatenate([before, value, after], axis=dim)
    return value


def from_behind(value, axis, by):
    devices = lax.axis_size(axis)
    return lax.ppermute(value, axis, [(i, (i + by) % devices) for i in range(devices)])


def side_masks(length):
    where = jnp.arange(length, dtype=jnp.int32)
    zpos = where % P_SIZE
    ypos = where // P_SIZE % P_SIZE
    return (
        (zpos < P_SIZE - 1).astype(jnp.float32),
        (zpos > 0).astype(jnp.float32),
        (ypos < P_SIZE - 1).astype(jnp.float32),
        (ypos > 0).astype(jnp.float32),
    )


def flat_stencil(padded, length, masks):
    plane = P_SIZE * P_SIZE
    values = padded[:, plane : plane + length]
    beside = padded[:, 2 * plane : 2 * plane + length] + padded[:, 0:length]
    beside = beside + masks[0] * padded[:, plane + 1 : plane + 1 + length]
    beside = beside + masks[1] * padded[:, plane - 1 : plane - 1 + length]
    beside = beside + masks[2] * padded[:, plane + P_SIZE : plane + P_SIZE + length]
    beside = beside + masks[3] * padded[:, plane - P_SIZE : plane - P_SIZE + length]
    return (values, 6.0 * values - beside)


def flat_hamiltonian(values, potential, masks):
    plane = P_SIZE * P_SIZE
    padded = jnp.pad(values, ((0, 0), (plane, plane)))
    middle_values, laplace = flat_stencil(padded, values.shape[1], masks)
    return laplace + potential * middle_values


def filtered_basis(orbitals, potential, kept_count, start_index):
    orbital_count = orbitals.shape[0]
    masks = side_masks(G)
    middle = 0.5 * (HIGH_EDGE + LOW_EDGE)
    spread = 0.5 * (HIGH_EDGE - LOW_EDGE)
    previous = orbitals.astype(jnp.float32)
    current = (flat_hamiltonian(previous, potential, masks) - middle * previous) / spread
    following = (
        2.0 * (flat_hamiltonian(current, potential, masks) - middle * current) / spread - previous
    )
    previous, current = (current, following)
    magnitude = jnp.sqrt(jnp.mean(current * current, axis=1, keepdims=True) + 1e-06)
    active = start_index + jnp.arange(orbital_count, dtype=jnp.int32) < kept_count
    return jnp.where(active[:, None], current / magnitude, 0.0).astype(jnp.bfloat16)


def slab_applied(slab_rows, slab_potential):
    length = slab_rows.shape[1]
    padded = with_halo(slab_rows, (("band", 1),), P_SIZE * P_SIZE).astype(jnp.float32)
    values, laplace = flat_stencil(padded, length, side_masks(length))
    return (laplace + slab_potential * values).astype(jnp.bfloat16)


def face_pair(gridded, axis_place, upper):
    extent = gridded.shape[axis_place]
    surface = lax.index_in_dim(gridded, extent - 1 if upper else 0, axis_place, keepdims=False)
    beneath = lax.index_in_dim(gridded, extent - 2 if upper else 1, axis_place, keepdims=False)
    return (surface, beneath)


def face_terms(own_surface, own_beneath, other_surface, other_beneath):
    own_slope = own_surface - own_beneath
    other_slope = other_surface - other_beneath
    leading = jnp.concatenate(
        [-PENALTY * own_surface + 0.5 * own_slope, 0.5 * own_surface], axis=-1
    )
    trailing = jnp.concatenate([other_surface, other_slope], axis=-1)
    return (leading, trailing)


def apply_blocks(terms, current):
    offsets = [0, 1, -1, EB, -EB]
    running = jnp.zeros((terms[0][0].shape[0], current.shape[1]), jnp.float32)
    for position, offset in enumerate(offsets):
        matrix, contract = terms[position]
        if offset == 0:
            source = current
        else:
            source = from_behind(current, "elem", -offset)
        running = running + lax.dot_general(
            matrix, source, (((contract,), (0,)), ((), ())), preferred_element_type=jnp.float32
        )
    return running


def scaled(terms, current):
    return (apply_blocks(terms, current) - SHIFT_CENTER * current.astype(jnp.float32)) / HALF_WIDTH


def on_device(orbitals, potential, basis_count, states):
    per_device = orbitals.shape[1]
    band_place = lax.axis_index("band")
    start_index = band_place * per_device
    basis = filtered_basis(orbitals[0], potential[0], basis_count[0], start_index)
    basis_rows = lax.all_to_all(basis, "band", split_axis=1, concat_axis=0, tiled=True)
    orbital_count = basis_rows.shape[0]
    slab_length = basis_rows.shape[1]
    planes = slab_length // (P_SIZE * P_SIZE)
    slab_potential = lax.dynamic_slice_in_dim(
        potential[0], band_place * slab_length, slab_length, 0
    )
    applied_rows = slab_applied(basis_rows, slab_potential)
    interior = lax.dot_general(
        basis_rows, applied_rows, (((1,), (1,)), ((), ())), preferred_element_type=jnp.float32
    ) * (1.0 / G)
    half_grid = basis_rows.reshape(orbital_count, planes, P_SIZE, P_SIZE)
    directions = [
        (1, 1, True, False),
        (-1, 1, False, True),
        (EB, 0, True, False),
        (-EB, 0, False, True),
    ]
    chosen = [directions[0], directions[2]]
    partials = [interior]
    for offset, axis_code, own_upper, other_upper in chosen:
        outgoing = jnp.stack(face_pair(half_grid, 2 + axis_code, other_upper))
        received = from_behind(outgoing, "elem", -offset)
        own_surface, own_beneath = face_pair(half_grid, 2 + axis_code, own_upper)
        leading, trailing = face_terms(
            own_surface.reshape(orbital_count, -1).astype(jnp.float32),
            own_beneath.reshape(orbital_count, -1).astype(jnp.float32),
            received[0].reshape(orbital_count, -1).astype(jnp.float32),
            received[1].reshape(orbital_count, -1).astype(jnp.float32),
        )
        partials.append(
            lax.dot_general(
                leading,
                trailing,
                (((1,), (1,)), ((), ())),
                precision=HIGHEST,
                preferred_element_type=jnp.float32,
            )
            * (1.0 / (P_SIZE * P_SIZE))
        )
    rounded = jnp.stack(partials).astype(jnp.bfloat16).astype(jnp.float32)
    summed = lax.psum(rounded.astype(jnp.bfloat16), "band")
    mirrored = []
    for position, offset in ((1, 1), (2, EB)):
        mirrored.append(from_behind(summed[position], "elem", offset))
    terms = [(summed[0], 1), (summed[1], 1), (mirrored[0], 0), (summed[2], 1), (mirrored[1], 0)]
    start_states = states[0]
    first_term = scaled(terms, start_states).astype(jnp.bfloat16)
    second_term = (2.0 * scaled(terms, first_term) - start_states.astype(jnp.float32)).astype(
        jnp.bfloat16
    )
    third_term = 2.0 * scaled(terms, second_term) - first_term.astype(jnp.float32)
    magnitude = jnp.sqrt(jnp.mean(third_term * third_term, axis=0, keepdims=True) + 1e-06)
    return (third_term / magnitude).astype(jnp.bfloat16)[None]


def solution(mesh):
    placed = (P("elem", "band", None), P("elem", None), P("elem"), P("elem", None, "band"))
    return jax.shard_map(
        on_device, mesh=mesh, in_specs=placed, out_specs=P("elem", None, "band"), check_vma=False
    )
```

profile of v0, /device:TPU:0, one launch (start us, length us, event | category | flops | bytes accessed | tf_op | source)
XLA Modules:
  0.0 395.8 jit_solution(10263629934132865185)
XLA Ops:
  7.9 4.9 %copy.11 = bf16[1,128,13824]{1,2,0:T(8,128)(2,1)S(1)} copy(bf16[1,128,13824]{2,1,0:T(8,128)(2,1)} %param.4) | data formatting | bytes 7077888 | tf_op args[0]
  12.8 3.1 bitcast_convert_fusion
  15.9 1.6 reduce
  18.4 30.3 %broadcast_multiply_fusion = (f32[128,13824]{0,1:T(8,128)S(1)}, f32[128,13824]{0,1:T(8,128)S(1)}) fusion(f32[13824]{0:T(1024)} %reduce, f32[13824]{0:T(1024)} %get-tuple-element.29, f32[13824]{0:T(1024)} %get-tuple-element.30, f32[13824]{0:T(1024)} %get-tuple-element.28, f32[13824]{0:T(1024)} %get-tuple-element.27, f32[128,13824]{0,1:T(8,128)} %bitcast_convert_fusion, ...), kind=kLoop, calls=%fused_computation.34 | loop fusion | flops 30081024 | bytes 25049088 | tf_op jit(solution)/shard_map/div | solution.py:73
  48.7 28.4 %multiply_reduce_fusion = (f32[128]{0:T(128)S(1)}, f32[128,13824]{0,1:T(8,128)}) fusion(bf16[1,128,13824]{1,2,0:T(8,128)(2,1)S(1)} %copy.11, f32[128,13824]{0,1:T(8,128)S(1)} %get-tuple-element.8, f32[13824]{0:T(1024)S(1)} %broadcast_multiply_fusion.1, f32[13824]{0:T(1024)S(1)} %copy-done.5, f32[13824]{0:T(1024)S(1)} %copy-done.6, f32[13824]{0:T(1024)S(1)} %copy-done.4, ...), kind=kLoop, calls=%fused_computation.20 | loop fusion | flops 35389312 | bytes 25049600 | tf_op jit(solution)/shard_map/reduce_sum | solution.py:78
  77.8 4.7 %select_convert_fusion = bf16[128,13824]{0,1:T(8,128)(2,1)} fusion(f32[128,13824]{0,1:T(8,128)} %get-tuple-element.6, f32[128]{0:T(128)S(1)} %add_sqrt_fusion.1, pred[128]{0:T(512)(128)(4,1)S(1)} %add_compare_fusion), kind=kLoop, calls=%fused_computation.19 | loop fusion | flops 5308416 | bytes 10617472 | tf_op jit(solution)/shard_map/convert_element_type | solution.py:80
  82.5 6.3 %all-to-all-start = ((bf16[128,4,3456]{0,2,1:T(8,128)(2,1)}), bf16[128,4,3456]{0,2,1:T(8,128)(2,1)S(1)}, u32[]{:S(2)}, u32[]{:S(2)}) async-start(bf16[128,4,3456]{0,2,1:T(8,128)(2,1)} %bitcast.98), calls=%async_computation | async-start | bytes 7077888 | tf_op jit(solution)/shard_map/all_to_all | solution.py:131
  88.8 1.4 dynamic-slice_reduce_fusion
  91.4 76.5 %all-to-all-done = bf16[128,4,3456]{0,2,1:T(8,128)(2,1)S(1)} async-done(((bf16[128,4,3456]{0,2,1:T(8,128)(2,1)}), bf16[128,4,3456]{0,2,1:T(8,128)(2,1)S(1)}, u32[]{:S(2)}, u32[]{:S(2)}) %all-to-all-start) | async-done | bytes 3538976 | tf_op jit(solution)/shard_map/all_to_all | solution.py:131
  167.9 4.0 %copy.12 = bf16[4,128,3456]{2,1,0:T(8,128)(2,1)} copy(bf16[4,128,3456]{1,2,0:T(8,128)(2,1)S(1)} %bitcast.93) | data formatting | bytes 7077888 | tf_op jit(solution)/shard_map/all_to_all | solution.py:131
  171.9 17.3 %copy.17 = bf16[4,128,3456]{1,0,2:T(4,128)(2,1)} copy(bf16[4,128,3456]{1,2,0:T(8,128)(2,1)S(1)} %bitcast.94) | data formatting | bytes 7077888 | tf_op jit(solution)/shard_map/all_to_all | solution.py:131
  189.2 7.1 %reshape.138 = bf16[512,6,24,24]{0,3,2,1:T(8,128)(2,1)} reshape(bf16[4,128,3456]{1,0,2:T(4,128)(2,1)} %copy.17) | data formatting | bytes 7077888 | tf_op jit(solution)/shard_map/reshape | solution.py:142
  196.4 3.3 fusion.98
  199.6 3.4 fusion.66
  203.0 1.7 slice_bitcast_fusion.7
  204.8 1.4 fusion.97
  206.2 2.1 copy.13
  208.3 2.1 collective-permute-start
  210.5 2.1 copy.14
  212.6 1.3 collective-permute-start.1
  213.9 1.0 copy.24
  214.9 1.0 copy.25
  215.9 1.3 collective-permute-start.2
  217.2 1.0 pad_maximum_fusion.2
  218.2 1.0 copy.18
  219.2 1.0 copy.19
  220.8 1.1 fusion.62
  222.0 6.6 %collective-permute-done.3 = bf16[2,512,6,24]{1,3,2,0:T(8,128)(2,1)S(1)} collective-permute-done((bf16[2,512,6,24]{1,3,2,0:T(8,128)(2,1)S(1)}, bf16[2,512,6,24]{1,3,2,0:T(8,128)(2,1)S(1)}, u32[]{:S(2)}, u32[]{:S(2)}) %collective-permute-start.3) | collective-permute-done | bytes 294944 | tf_op jit(solution)/shard_map/ppermute | solution.py:34
  228.6 2.7 fusion.27
  231.4 2.7 fusion.26
  234.0 2.2 copy.15
  236.2 2.2 copy.16
  238.4 8.4 %concatenate.15 = bf16[512,4608]{1,0:T(8,128)(2,1)} concatenate(bf16[512,576]{1,0:T(8,128)(2,1)} %copy.15, bf16[512,3456]{1,0:T(8,128)(2,1)S(1)} %bitcast.96, bf16[512,576]{1,0:T(8,128)(2,1)} %copy.16), dimensions={1} | concatenate | bytes 9437184 | tf_op jit(solution)/shard_map/concatenate | solution.py:28
  246.8 7.2 %convert_element_type.152 = f32[512,4608]{1,0:T(8,128)} convert(bf16[512,4608]{1,0:T(8,128)(2,1)} %concatenate.15) | non-fusion elementwise | flops 2359296 | bytes 14155776 | tf_op jit(solution)/shard_map/convert_element_type | solution.py:85
  254.0 22.0 %fusion.28 = bf16[1,512,512]{2,1,0:T(8,128)(2,1)} fusion(bf16[512,3456]{1,0:T(8,128)(2,1)S(1)} %bitcast.97, f32[512,4608]{1,0:T(8,128)} %convert_element_type.152, f32[3456]{0:T(1024)} %dynamic-slice_reduce_fusion, f32[3456]{0:T(1024)} %get-tuple-element.33, f32[3456]{0:T(1024)} %get-tuple-element.34, f32[3456]{0:T(1024)} %get-tuple-element.32, ...), kind=kOutput, calls=%fused_computation.45 | convolution fusion | flops 1837236224 | bytes 53687808 | tf_op jit(solution)/shard_map/dot_general | solution.py:139
  276.1 2.7 pad_maximum_fusion
  278.8 2.1 collective-permute-start.4
  281.4 69.0 %all-reduce.4.cloned.1.call-done = bf16[3,512,512]{2,1,0:T(8,128)(2,1)} async-done(((bf16[3,512,512]{2,1,0:T(8,128)(2,1)}), bf16[3,512,512]{2,1,0:T(8,128)(2,1)}) %all-reduce.4.cloned.1.call-update) | async-done | bytes 1572880 | tf_op jit(solution)/shard_map/psum | solution.py:172
  350.4 1.4 slice_bitcast_fusion.1
  351.8 1.5 collective-permute-start.8
  353.4 1.4 fusion.61
  354.7 1.3 fusion.95
  356.1 1.3 convolution_add_fusion.5
  357.4 12.6 %collective-permute-done.8 = bf16[512,512]{1,0:T(8,128)(2,1)S(1)} collective-permute-done((bf16[512,512]{1,0:T(8,128)(2,1)S(1)}, bf16[512,512]{1,0:T(8,128)(2,1)S(1)}, u32[]{:S(2)}, u32[]{:S(2)}) %collective-permute-start.8) | collective-permute-done | bytes 524320 | tf_op jit(solution)/shard_map/ppermute | solution.py:34
  370.9 1.5 collective-permute-start.11
  372.9 5.3 %collective-permute-done.11 = bf16[512,128]{1,0:T(8,128)(2,1)S(1)} collective-permute-done((bf16[512,128]{1,0:T(8,128)(2,1)S(1)}, bf16[512,128]{1,0:T(8,128)(2,1)S(1)}, u32[]{:S(2)}, u32[]{:S(2)}) %collective-permute-start.11) | collective-permute-done | bytes 131104 | tf_op jit(solution)/shard_map/ppermute | solution.py:34
  379.6 1.5 collective-permute-start.14
  381.6 5.3 %collective-permute-done.14 = bf16[512,128]{1,0:T(8,128)(2,1)S(1)} collective-permute-done((bf16[512,128]{1,0:T(8,128)(2,1)S(1)}, bf16[512,128]{1,0:T(8,128)(2,1)S(1)}, u32[]{:S(2)}, u32[]{:S(2)}) %collective-permute-start.14) | collective-permute-done | bytes 131104 | tf_op jit(solution)/shard_map/ppermute | solution.py:34
  (63 shorter events, 9.8 us)
Async XLA Ops:
  18.3 30.3 %copy-start.3 = (f32[13824]{0:T(1024)S(1)}, f32[13824]{0:T(1024)}, u32[]{:S(2)}) copy-start(f32[13824]{0:T(1024)} %get-tuple-element.27) | copy-start | bytes 165892
  18.3 30.3 %copy-start.4 = (f32[13824]{0:T(1024)S(1)}, f32[13824]{0:T(1024)}, u32[]{:S(2)}) copy-start(f32[13824]{0:T(1024)} %get-tuple-element.28) | copy-start | bytes 165892
  18.3 30.3 %copy-start.5 = (f32[13824]{0:T(1024)S(1)}, f32[13824]{0:T(1024)}, u32[]{:S(2)}) copy-start(f32[13824]{0:T(1024)} %get-tuple-element.29) | copy-start | bytes 165892
  18.4 30.3 %copy-start.6 = (f32[13824]{0:T(1024)S(1)}, f32[13824]{0:T(1024)}, u32[]{:S(2)}) copy-start(f32[13824]{0:T(1024)} %get-tuple-element.30) | copy-start | bytes 165892
  82.5 85.4 %all-to-all-start = ((bf16[128,4,3456]{0,2,1:T(8,128)(2,1)}), bf16[128,4,3456]{0,2,1:T(8,128)(2,1)S(1)}, u32[]{:S(2)}, u32[]{:S(2)}) async-start(bf16[128,4,3456]{0,2,1:T(8,128)(2,1)} %bitcast.98), calls=%async_computation | async-start | bytes 7077888 | tf_op jit(solution)/shard_map/all_to_all | solution.py:131
  88.8 261.6 %all-reduce.4.cloned.1.call-start = ((), (), s32[]{:S(2)}) async-start(), calls=%async_computation.1 | async-start | bytes 3145728 | tf_op jit(solution)/shard_map/psum | solution.py:172
  189.2 15.5 %copy-start.1 = (bf16[4,128,3456]{2,1,0:T(8,128)(2,1)S(1)}, bf16[4,128,3456]{2,1,0:T(8,128)(2,1)}, u32[]{:S(2)}) copy-start(bf16[4,128,3456]{2,1,0:T(8,128)(2,1)} %copy.12) | copy-start | bytes 10616836
  208.3 25.7 %collective-permute-start = (bf16[512,576]{0,1:T(8,128)(2,1)}, bf16[512,576]{0,1:T(8,128)(2,1)}, u32[]{:S(2)}, u32[]{:S(2)}) collective-permute-start(bf16[512,576]{0,1:T(8,128)(2,1)} %copy.13), channel_id=1, source_target_pairs={{0,1},{1,2},{2,3},{4,5},{5,6},{6,7},{8,9},{9,10},{10,11},{12,13},{... | collective-permute-start | bytes 1769480 | tf_op jit(solution)/shard_map/ppermute | solution.py:26
  212.6 23.6 %collective-permute-start.1 = (bf16[512,576]{0,1:T(8,128)(2,1)}, bf16[512,576]{0,1:T(8,128)(2,1)}, u32[]{:S(2)}, u32[]{:S(2)}) collective-permute-start(bf16[512,576]{0,1:T(8,128)(2,1)} %copy.14), channel_id=1, source_target_pairs={{1,0},{2,1},{3,2},{5,4},{6,5},{7,6},{9,8},{10,9},{11,10},{13,12},{... | collective-permute-start | bytes 1769480 | tf_op jit(solution)/shard_map/ppermute | solution.py:27
  215.9 6.0 %collective-permute-start.2 = (bf16[2,512,6,24]{1,3,2,0:T(8,128)(2,1)S(1)}, bf16[2,512,6,24]{1,3,2,0:T(8,128)(2,1)S(1)}, u32[]{:S(2)}, u32[]{:S(2)}) collective-permute-start(bf16[2,512,6,24]{1,3,2,0:T(8,128)(2,1)S(1)} %pad_maximum_fusion.1), channel_id=1, source_target_pairs={{0,28},{4,0},{8,4},{12,8},{16,12},{20,16},{24,20},{28,24},{1,29},{... | collective-permute-start | bytes 884744 | tf_op jit(solution)/shard_map/ppermute | solution.py:34
  220.2 8.4 %collective-permute-start.3 = (bf16[2,512,6,24]{1,3,2,0:T(8,128)(2,1)S(1)}, bf16[2,512,6,24]{1,3,2,0:T(8,128)(2,1)S(1)}, u32[]{:S(2)}, u32[]{:S(2)}) collective-permute-start(bf16[2,512,6,24]{1,3,2,0:T(8,128)(2,1)S(1)} %pad_maximum_fusion.2), channel_id=1, source_target_pairs={{0,16},{4,20},{8,24},{12,28},{16,0},{20,4},{24,8},{28,12},{1,17},{... | collective-permute-start | bytes 884744 | tf_op jit(solution)/shard_map/ppermute | solution.py:34
  276.0 94.4 %copy-start.2 = (bf16[1,512,128]{2,1,0:T(8,128)(2,1)S(1)}, bf16[1,512,128]{2,1,0:T(8,128)(2,1)}, u32[]{:S(2)}) copy-start(bf16[1,512,128]{2,1,0:T(8,128)(2,1)} %param.7) | copy-start | bytes 393220
  278.8 77.3 %collective-permute-start.4 = (bf16[512,128]{1,0:T(8,128)(2,1)}, bf16[512,128]{1,0:T(8,128)(2,1)S(1)}, u32[]{:S(2)}, u32[]{:S(2)}) collective-permute-start(bf16[512,128]{1,0:T(8,128)(2,1)} %bitcast.99), channel_id=1, source_target_pairs={{0,28},{4,0},{8,4},{12,8},{16,12},{20,16},{24,20},{28,24},{1,29},{... | collective-permute-start | bytes 393224 | tf_op jit(solution)/shard_map/ppermute | solution.py:34
  280.9 73.8 %collective-permute-start.7 = (bf16[512,128]{1,0:T(8,128)(2,1)}, bf16[512,128]{1,0:T(8,128)(2,1)S(1)}, u32[]{:S(2)}, u32[]{:S(2)}) collective-permute-start(bf16[512,128]{1,0:T(8,128)(2,1)} %bitcast.100), channel_id=1, source_target_pairs={{0,16},{4,20},{8,24},{12,28},{16,0},{20,4},{24,8},{28,12},{1,17},{... | collective-permute-start | bytes 393224 | tf_op jit(solution)/shard_map/ppermute | solution.py:34
  281.4 89.0 %collective-permute-start.6 = (bf16[512,128]{1,0:T(8,128)(2,1)}, bf16[512,128]{1,0:T(8,128)(2,1)S(1)}, u32[]{:S(2)}, u32[]{:S(2)}) collective-permute-start(bf16[512,128]{1,0:T(8,128)(2,1)} %bitcast.101), channel_id=1, source_target_pairs={{0,4},{4,8},{8,12},{12,16},{16,20},{20,24},{24,28},{28,0},{1,5},{5... | collective-permute-start | bytes 393224 | tf_op jit(solution)/shard_map/ppermute | solution.py:34
  350.4 22.1 %copy-start = (bf16[3,512,512]{2,1,0:T(8,128)(2,1)S(1)}, bf16[3,512,512]{2,1,0:T(8,128)(2,1)}, u32[]{:S(2)}) copy-start(bf16[3,512,512]{2,1,0:T(8,128)(2,1)} %all-reduce.4.cloned.1.call-done) | copy-start | bytes 4718596
  351.8 18.2 %collective-permute-start.8 = (bf16[512,512]{1,0:T(8,128)(2,1)S(1)}, bf16[512,512]{1,0:T(8,128)(2,1)S(1)}, u32[]{:S(2)}, u32[]{:S(2)}) collective-permute-start(bf16[512,512]{1,0:T(8,128)(2,1)S(1)} %get-tuple-element.20), channel_id=1, source_target_pairs={{0,16},{4,20},{8,24},{12,28},{16,0},{20,4},{24,8},{28,12},{1,17},{... | collective-permute-start | bytes 1572872 | tf_op jit(solution)/shard_map/ppermute | solution.py:34
  353.4 17.1 %collective-permute-start.5 = (bf16[512,512]{1,0:T(8,128)(2,1)S(1)}, bf16[512,512]{1,0:T(8,128)(2,1)S(1)}, u32[]{:S(2)}, u32[]{:S(2)}) collective-permute-start(bf16[512,512]{1,0:T(8,128)(2,1)S(1)} %get-tuple-element.19), channel_id=1, source_target_pairs={{0,4},{4,8},{8,12},{12,16},{16,20},{20,24},{24,28},{28,0},{1,5},{5... | collective-permute-start | bytes 1572872 | tf_op jit(solution)/shard_map/ppermute | solution.py:34
  370.8 7.7 %collective-permute-start.9 = (bf16[512,128]{1,0:T(8,128)(2,1)S(1)}, bf16[512,128]{1,0:T(8,128)(2,1)S(1)}, u32[]{:S(2)}, u32[]{:S(2)}) collective-permute-start(bf16[512,128]{1,0:T(8,128)(2,1)S(1)} %fusion.46), channel_id=1, source_target_pairs={{0,28},{4,0},{8,4},{12,8},{16,12},{20,16},{24,20},{28,24},{1,29},{... | collective-permute-start | bytes 393224 | tf_op jit(solution)/shard_map/ppermute | solution.py:34
  370.9 7.3 %collective-permute-start.11 = (bf16[512,128]{1,0:T(8,128)(2,1)S(1)}, bf16[512,128]{1,0:T(8,128)(2,1)S(1)}, u32[]{:S(2)}, u32[]{:S(2)}) collective-permute-start(bf16[512,128]{1,0:T(8,128)(2,1)S(1)} %fusion.46), channel_id=1, source_target_pairs={{0,16},{4,20},{8,24},{12,28},{16,0},{20,4},{24,8},{28,12},{1,17},{... | collective-permute-start | bytes 393224 | tf_op jit(solution)/shard_map/ppermute | solution.py:34
  372.4 6.7 %collective-permute-start.10 = (bf16[512,128]{1,0:T(8,128)(2,1)S(1)}, bf16[512,128]{1,0:T(8,128)(2,1)S(1)}, u32[]{:S(2)}, u32[]{:S(2)}) collective-permute-start(bf16[512,128]{1,0:T(8,128)(2,1)S(1)} %fusion.46), channel_id=1, source_target_pairs={{0,4},{4,8},{8,12},{12,16},{16,20},{20,24},{24,28},{28,0},{1,5},{5... | collective-permute-start | bytes 393224 | tf_op jit(solution)/shard_map/ppermute | solution.py:34
  379.5 7.7 %collective-permute-start.12 = (bf16[512,128]{1,0:T(8,128)(2,1)S(1)}, bf16[512,128]{1,0:T(8,128)(2,1)S(1)}, u32[]{:S(2)}, u32[]{:S(2)}) collective-permute-start(bf16[512,128]{1,0:T(8,128)(2,1)S(1)} %fusion.45), channel_id=1, source_target_pairs={{0,28},{4,0},{8,4},{12,8},{16,12},{20,16},{24,20},{28,24},{1,29},{... | collective-permute-start | bytes 393224 | tf_op jit(solution)/shard_map/ppermute | solution.py:34
  379.6 7.3 %collective-permute-start.14 = (bf16[512,128]{1,0:T(8,128)(2,1)S(1)}, bf16[512,128]{1,0:T(8,128)(2,1)S(1)}, u32[]{:S(2)}, u32[]{:S(2)}) collective-permute-start(bf16[512,128]{1,0:T(8,128)(2,1)S(1)} %fusion.45), channel_id=1, source_target_pairs={{0,16},{4,20},{8,24},{12,28},{16,0},{20,4},{24,8},{28,12},{1,17},{... | collective-permute-start | bytes 393224 | tf_op jit(solution)/shard_map/ppermute | solution.py:34
  381.1 6.7 %collective-permute-start.13 = (bf16[512,128]{1,0:T(8,128)(2,1)S(1)}, bf16[512,128]{1,0:T(8,128)(2,1)S(1)}, u32[]{:S(2)}, u32[]{:S(2)}) collective-permute-start(bf16[512,128]{1,0:T(8,128)(2,1)S(1)} %fusion.45), channel_id=1, source_target_pairs={{0,4},{4,8},{8,12},{12,16},{16,20},{20,24},{24,28},{28,0},{1,5},{5... | collective-permute-start | bytes 393224 | tf_op jit(solution)/shard_map/ppermute | solution.py:34
Sparse Core Ops, SparseCore 0:
  278.9 71.4 all-reduce.3
where the time goes:
time: 397 us; the launch traced here: 396 us
  waiting for transfers between devices  175 us (44%)
  other arithmetic  87.9 us (22%)
  local copies, waits for them, and re-layouts  63.5 us (16%)
  matrix products  35.2 us (9%)
  starting transfers between devices  19.3 us (5%)
  between operations  14.4 us (4%)
    all_to_all x1, waiting for transfers between devices, on_device(): lax.all_to_all(basis, 'band', split_axis=1, concat_axis=0, tiled=True)  76.5 us
    psum x1, waiting for transfers between devices, on_device(): summed = lax.psum(rounded.astype(jnp.bfloat16), 'band')  69 us
    div x1, other arithmetic, filtered_basis(): (flat_hamiltonian(previous, potential, masks) - middle * previous) / spread  30.3 us
    ppermute x13, waiting for transfers between devices, from_behind(): lax.ppermute(value, axis, [(i, (i + by) % devices) for i in range(devices)])  29.9 us
    reduce_sum x1, other arithmetic, filtered_basis(): jnp.mean(current * current, axis=1, keepdims=True) + 1e-06  28.4 us
    dot_general x1, matrix products, on_device(): lax.dot_general(basis_rows, applied_rows, (((1,), (1,)), ((), ())), prefe...  22 us
    all_to_all x2, local copies, waits for them, and re-layouts, on_device(): lax.all_to_all(basis, 'band', split_axis=1, concat_axis=0, tiled=True)  21.3 us
    ppermute x13, starting transfers between devices, from_behind(): lax.ppermute(value, axis, [(i, (i + by) % devices) for i in range(devices)])  9.59 us
  transfers between devices with their start and end apart: 17, of which 6 were waited for; matrix products, arithmetic and copies ran while one was open for 7% of the time, Pallas kernels for 0%

commit v1 on v0

v1 whole, which is shorter than its diff:
```python
import functools

import jax
import jax.numpy as jnp
from jax import lax
from jax.experimental import pallas as pl
from jax.experimental.pallas import tpu as pltpu
from jax.sharding import PartitionSpec as P

P_SIZE = 24
G = 13824
EB = 4
PLANE = P_SIZE * P_SIZE
PAD = 640
ROWS = 16


LOW_EDGE = 4.0
HIGH_EDGE = 14.0
SHIFT_CENTER = 4.0
HALF_WIDTH = 6.0
VMEM_LIMIT = 48 * 1024 * 1024
NT = (((1,), (1,)), ((), ()))


def from_behind(value, axis, by):
    devices = lax.axis_size(axis)
    return lax.ppermute(value, axis, [(i, (i + by) % devices) for i in range(devices)])


def side_masks(length):
    where = jnp.arange(length, dtype=jnp.int32)
    zpos = where % P_SIZE
    ypos = where // P_SIZE % P_SIZE
    return jnp.stack(
        [
            (zpos < P_SIZE - 1).astype(jnp.float32),
            (zpos > 0).astype(jnp.float32),
            (ypos < P_SIZE - 1).astype(jnp.float32),
            (ypos > 0).astype(jnp.float32),
        ]
    )


def lane_chunks(length):
    step = 1152
    return [(at, min(step, length - at)) for at in range(0, length, step)]


def neighbour_sum(ref, masks_ref, at, size):
    base = PAD + at

    def shifted(by):
        return ref[:, base + by : base + by + size]

    def mask(which):
        return masks_ref[which : which + 1, at : at + size]

    total = shifted(PLANE) + shifted(-PLANE)
    total = total + mask(0) * shifted(1) + mask(1) * shifted(-1)
    return total + mask(2) * shifted(P_SIZE) + mask(3) * shifted(-P_SIZE)


def clear_pads(ref, length):
    ref[:, 0:PAD] = jnp.zeros((ref.shape[0], PAD), jnp.float32)
    ref[:, PAD + length :] = jnp.zeros((ref.shape[0], ref.shape[1] - PAD - length), jnp.float32)


def filter_kernel(slabs, bounds_ref, orbitals_ref, diag_ref, masks_ref, out_ref, first_ref, second_ref):
    spread = 0.5 * (HIGH_EDGE - LOW_EDGE)
    rows, length = orbitals_ref.shape

    @pl.when(pl.program_id(0) == 0)
    def _():
        clear_pads(first_ref, length)
        clear_pads(second_ref, length)

    first_ref[:, PAD : PAD + length] = orbitals_ref[...].astype(jnp.float32)
    for at, size in lane_chunks(length):
        diag = diag_ref[0:1, at : at + size]
        own = first_ref[:, PAD + at : PAD + at + size]
        second_ref[:, PAD + at : PAD + at + size] = diag * own - neighbour_sum(
            first_ref, masks_ref, at, size
        ) * (1.0 / spread)
    squares = jnp.zeros((rows, 1), jnp.float32)
    for at, size in lane_chunks(length):
        diag = diag_ref[0:1, at : at + size]
        own = second_ref[:, PAD + at : PAD + at + size]
        previous = first_ref[:, PAD + at : PAD + at + size]
        value = (
            2.0 * diag * own
            - neighbour_sum(second_ref, masks_ref, at, size) * (2.0 / spread)
            - previous
        )
        first_ref[:, PAD + at : PAD + at + size] = value
        squares = squares + jnp.sum(value * value, axis=1, keepdims=True)
    scale = 1.0 / jnp.sqrt(squares * (1.0 / length) + 1e-06)
    row = bounds_ref[1] + pl.program_id(0) * rows + lax.broadcasted_iota(jnp.int32, (rows, 1), 0)
    scale = jnp.where(row < bounds_ref[0], scale, 0.0)
    share = length // slabs
    for slab in range(slabs):
        start = PAD + slab * share
        out_ref[slab] = (first_ref[:, start : start + share] * scale).astype(jnp.bfloat16)


def filtered_basis(orbitals, potential, kept_count, start_index, slabs):
    count, length = orbitals.shape
    middle = 0.5 * (HIGH_EDGE + LOW_EDGE)
    spread = 0.5 * (HIGH_EDGE - LOW_EDGE)
    diag = ((6.0 - middle) + potential)[None] / spread
    bounds = jnp.stack([kept_count, start_index]).astype(jnp.int32)
    return pl.pallas_call(
        functools.partial(filter_kernel, slabs),
        grid=(count // ROWS,),
        in_specs=[
            pl.BlockSpec(memory_space=pltpu.SMEM),
            pl.BlockSpec((ROWS, length), lambda i: (i, 0)),
            pl.BlockSpec((1, length), lambda i: (0, 0)),
            pl.BlockSpec((4, length), lambda i: (0, 0)),
        ],
        out_specs=pl.BlockSpec((slabs, ROWS, length // slabs), lambda i: (0, i, 0)),
        out_shape=jax.ShapeDtypeStruct((slabs, count, length // slabs), jnp.bfloat16),
        scratch_shapes=[pltpu.VMEM((ROWS, length + 2 * PAD), jnp.float32)] * 2,
        compiler_params=pltpu.CompilerParams(vmem_limit_bytes=VMEM_LIMIT),
    )(bounds, orbitals, diag, side_masks(length))


def face_chunk(length):
    return 1152 if length % 1152 == 0 else length


def face_selector(chunk):
    points = chunk // P_SIZE
    group = (2 * points + 127) // 128 * 128
    where = jnp.arange(chunk, dtype=jnp.int32)[:, None]
    zpos, ypos, xpos = where % P_SIZE, where // P_SIZE % P_SIZE, where // PLANE
    column = jnp.arange(group, dtype=jnp.int32)[None]
    point, late = column % points, column >= points
    used = column < 2 * points
    top = P_SIZE - 1
    layers = [(top - 1, top), (0, 1)]
    parts = []
    for pos, spot in ((zpos, where // P_SIZE), (ypos, xpos * P_SIZE + zpos)):
        for early_layer, late_layer in layers:
            layer = jnp.where(late, late_layer, early_layer)
            parts.append(((spot == point) & (pos == layer) & used).astype(jnp.bfloat16))
    return jnp.concatenate(parts, axis=1)


def faces_kernel(rows_ref, select_ref, lz_ref, rz_ref, ly_ref, ry_ref):
    chunk = select_ref.shape[0]
    group = select_ref.shape[1] // 4
    for which in range(rows_ref.shape[1] // chunk):
        picked = jnp.dot(
            rows_ref[:, which * chunk : (which + 1) * chunk],
            select_ref[...],
            preferred_element_type=jnp.float32,
        ).astype(jnp.bfloat16)
        for place, out in enumerate((lz_ref, rz_ref, ly_ref, ry_ref)):
            out[:, which * group : (which + 1) * group] = picked[:, place * group : (place + 1) * group]


def face_layers(rows):
    count, length = rows.shape
    chunk = face_chunk(length)
    select = face_selector(chunk)
    width = length // chunk * (select.shape[1] // 4)
    step = count // 4
    return pl.pallas_call(
        faces_kernel,
        grid=(4,),
        in_specs=[
            pl.BlockSpec((step, length), lambda i: (i, 0)),
            pl.BlockSpec(select.shape, lambda i: (0, 0)),
        ],
        out_specs=[pl.BlockSpec((step, width), lambda i: (i, 0))] * 4,
        out_shape=[jax.ShapeDtypeStruct((count, width), jnp.bfloat16)] * 4,
        compiler_params=pltpu.CompilerParams(vmem_limit_bytes=VMEM_LIMIT),
    )(rows, select)


def interior_kernel(all_ref, rows_ref, diag_ref, masks_ref, out_ref, wide_ref, applied_ref):
    count, length = rows_ref.shape

    @pl.when(pl.program_id(0) == 0)
    def _():
        clear_pads(wide_ref, length)

    @pl.loop(0, count // ROWS)
    def _(block):
        here = pl.ds(pl.multiple_of(block * ROWS, ROWS), ROWS)
        wide_ref[:, PAD : PAD + length] = rows_ref[here, :].astype(jnp.float32)
        for at, size in lane_chunks(length):
            own = wide_ref[:, PAD + at : PAD + at + size]
            applied_ref[here, at : at + size] = (
                diag_ref[0:1, at : at + size] * own - neighbour_sum(wide_ref, masks_ref, at, size)
            ).astype(jnp.bfloat16)

    out_ref[...] = lax.dot_general(
        applied_ref[...], all_ref[...], NT, preferred_element_type=jnp.float32
    )


def interior_block(rows, slab_potential):
    count, length = rows.shape
    step = count // 4
    return pl.pallas_call(
        interior_kernel,
        grid=(4,),
        in_specs=[
            pl.BlockSpec((count, length), lambda i: (0, 0)),
            pl.BlockSpec((step, length), lambda i: (i, 0)),
            pl.BlockSpec((1, length), lambda i: (0, 0)),
            pl.BlockSpec((4, length), lambda i: (0, 0)),
        ],
        out_specs=pl.BlockSpec((step, count), lambda i: (i, 0)),
        out_shape=jax.ShapeDtypeStruct((count, count), jnp.float32),
        scratch_shapes=[
            pltpu.VMEM((ROWS, length + 2 * PAD), jnp.float32),
            pltpu.VMEM((step, length), jnp.bfloat16),
        ],
        compiler_params=pltpu.CompilerParams(vmem_limit_bytes=VMEM_LIMIT),
    )(rows, rows, (6.0 + slab_potential)[None], side_masks(length))


def partials_kernel(inner_ref, near_ref, far_ref, lz_ref, rz_ref, ly_ref, ry_ref, out_ref):
    def product(a, b):
        return lax.dot_general(a, b, NT, preferred_element_type=jnp.float32)

    half = PLANE // 2
    seam = product(near_ref[...], far_ref[...])
    out_ref[0] = ((inner_ref[...] - seam) * (1.0 / G)).astype(jnp.bfloat16)
    weight = -0.5 / PLANE
    out_ref[1] = (product(lz_ref[...], rz_ref[...]) * weight).astype(jnp.bfloat16)
    out_ref[2] = (product(ly_ref[...], ry_ref[...]) * weight).astype(jnp.bfloat16)


def partial_blocks(inner, near, far, lz, rz, ly, ry):
    count = inner.shape[0]
    step = count // 4

    def cut(value):
        return pl.BlockSpec((step, value.shape[1]), lambda i: (i, 0))

    def full(value):
        return pl.BlockSpec(value.shape, lambda i: (0, 0))

    return pl.pallas_call(
        partials_kernel,
        grid=(4,),
        in_specs=[cut(inner), cut(near), full(far), cut(lz), full(rz), cut(ly), full(ry)],
        out_specs=pl.BlockSpec((3, step, count), lambda i: (0, i, 0)),
        out_shape=jax.ShapeDtypeStruct((3, count, count), jnp.bfloat16),
        compiler_params=pltpu.CompilerParams(vmem_limit_bytes=VMEM_LIMIT),
    )(inner, near, far, lz, rz, ly, ry)


def apply_blocks(terms, current):
    offsets = [0, 1, -1, EB, -EB]
    running = jnp.zeros((terms[0][0].shape[0], current.shape[1]), jnp.float32)
    for position, offset in enumerate(offsets):
        matrix, contract = terms[position]
        if offset == 0:
            source = current
        else:
            source = from_behind(current, "elem", -offset)
        running = running + lax.dot_general(
            matrix, source, (((contract,), (0,)), ((), ())), preferred_element_type=jnp.float32
        )
    return running


def scaled(terms, current):
    return (apply_blocks(terms, current) - SHIFT_CENTER * current.astype(jnp.float32)) / HALF_WIDTH


def summed_blocks(partials):
    return lax.psum(partials, "band")


def on_device(orbitals, potential, basis_count, states):
    per_device = orbitals.shape[1]
    slabs = lax.axis_size("band")
    band_place = lax.axis_index("band")
    start_index = band_place * per_device
    basis = filtered_basis(orbitals[0], potential[0], basis_count[0], start_index, slabs)
    basis_rows = lax.all_to_all(basis, "band", split_axis=0, concat_axis=0, tiled=True)
    basis_rows = basis_rows.reshape(slabs * per_device, -1)
    slab_length = basis_rows.shape[1]
    slab_potential = lax.dynamic_slice_in_dim(
        potential[0], band_place * slab_length, slab_length, 0
    )
    half = PLANE // 2
    initial, last = basis_rows[:, :PLANE], basis_rows[:, slab_length - PLANE :]
    up = [(i, i + 1) for i in range(slabs - 1)]
    down = [(j, i) for i, j in up]
    after = lax.ppermute(initial[:, :half], "band", down)
    before = lax.ppermute(last[:, half:], "band", up)
    lz, rz, ly, ry = face_layers(basis_rows)
    rz = from_behind(rz, "elem", -1)
    ry = from_behind(ry, "elem", -EB)
    inner = interior_block(basis_rows, slab_potential)
    near = jnp.concatenate([last[:, :half], after, initial[:, half:], before], axis=1)
    far = jnp.concatenate([after, last[:, :half], before, initial[:, half:]], axis=1)
    partials = partial_blocks(inner, near, far, lz, rz, ly, ry)
    summed = summed_blocks(partials)
    mirrored = []
    for position, offset in ((1, 1), (2, EB)):
        mirrored.append(from_behind(summed[position], "elem", offset))
    terms = [(summed[0], 1), (summed[1], 1), (mirrored[0], 0), (summed[2], 1), (mirrored[1], 0)]
    start_states = states[0]
    first_term = scaled(terms, start_states).astype(jnp.bfloat16)
    second_term = (2.0 * scaled(terms, first_term) - start_states.astype(jnp.float32)).astype(
        jnp.bfloat16
    )
    third_term = 2.0 * scaled(terms, second_term) - first_term.astype(jnp.float32)
    magnitude = jnp.sqrt(jnp.mean(third_term * third_term, axis=0, keepdims=True) + 1e-06)
    return (third_term / magnitude).astype(jnp.bfloat16)[None]


def solution(mesh):
    placed = (P("elem", "band", None), P("elem", None), P("elem"), P("elem", None, "band"))
    return jax.shard_map(
        on_device, mesh=mesh, in_specs=placed, out_specs=P("elem", None, "band"), check_vma=False
    )
```

time: 397 us -> 373 us (0.940)
  Pallas kernels: 0 us -> 140 us
  other arithmetic: 87.9 us -> 7.08 us
  local copies, waits for them, and re-layouts: 63.5 us -> 18.1 us
  matrix products: 35.2 us -> 4.73 us
  waiting for transfers between devices: 175 us -> 166 us
    pallas_call x0 -> x4, Pallas kernels: none -> 140 us  [the longest x1 90 us: filtered_basis(): pl.pallas_call(functools.partial(filter_kernel, slabs), grid=(count // RO...]
    div x1, other arithmetic: 30.3 us -> 0.89 us  [filtered_basis(): diag = (6.0 - middle + potential)[None] / spread]
    reduce_sum x1 -> x0, other arithmetic: 28.4 us -> none  [filtered_basis(): jnp.mean(current * current, axis=1, keepdims=True) + 1e-06]
    dot_general x3 -> x0, matrix products: 27.4 us -> none  [the longest x1 22 us: on_device(): lax.dot_general(basis_rows, applied_rows, (((1,), (1,)), ((), ())), prefe...]
    all_to_all x2 -> x0, local copies, waits for them, and re-layouts: 21.3 us -> none  [on_device(): lax.all_to_all(basis, 'band', split_axis=1, concat_axis=0, tiled=True)]
    convert_element_type x9 -> x0, other arithmetic: 17.7 us -> none  [the longest x1 7.24 us: slab_applied(): with_halo(slab_rows, (('band', 1),), P_SIZE * P_SIZE).astype(jnp.float32)]
    slice x6 -> x1, local copies, waits for them, and re-layouts: 9 us -> 1.36 us  [on_device(): before = lax.ppermute(last[:, half:], 'band', up)]
    reshape x1 -> x0, local copies, waits for them, and re-layouts: 7.12 us -> none  [on_device(): half_grid = basis_rows.reshape(orbital_count, planes, P_SIZE, P_SIZE)]
  transfers between devices with their start and end apart: 17 -> 17, of which waited for: 6 -> 7; matrix products, arithmetic and copies ran while one was open for 7% -> 4% of each run, Pallas kernels for 0% -> 11%
where the time goes in v1:
time: 373 us
  waiting for transfers between devices  166 us (45%)
  Pallas kernels  140 us (38%)
  starting transfers between devices  22.4 us (6%)
  local copies, waits for them, and re-layouts  18.1 us (5%)
  between operations  14.4 us (4%)
  other arithmetic  7.08 us (2%)
  matrix products  4.73 us (1%)
    pallas_call x1, Pallas kernels, filtered_basis(): pl.pallas_call(functools.partial(filter_kernel, slabs), grid=(count // RO...  90 us
    all_to_all x1, waiting for transfers between devices, on_device(): lax.all_to_all(basis, 'band', split_axis=0, concat_axis=0, tiled=True)  75.6 us
    psum x1, waiting for transfers between devices, summed_blocks(): return lax.psum(partials, 'band')  65.5 us
    pallas_call x1, Pallas kernels, interior_block(): pl.pallas_call(interior_kernel, grid=(4,), in_specs=[pl.BlockSpec((count,...  39.7 us
    ppermute x13, waiting for transfers between devices, from_behind(): lax.ppermute(value, axis, [(i, (i + by) % devices) for i in range(devices)])  24.9 us
    ppermute x13, starting transfers between devices, from_behind(): lax.ppermute(value, axis, [(i, (i + by) % devices) for i in range(devices)])  13.5 us
    unnamed x30, local copies, waits for them, and re-layouts  9.75 us
  transfers between devices with their start and end apart: 17, of which 7 were waited for; matrix products, arithmetic and copies ran while one was open for 4% of the time, Pallas kernels for 11%

profile of v1, /device:TPU:0, one launch (start us, length us, event | category | flops | bytes accessed | tf_op | source)
XLA Modules:
  0.0 372.7 jit_solution(11837253833362073044)
XLA Ops:
  6.5 0.5 broadcast_compare_fusion.2
  7.0 0.5 broadcast_compare_fusion
  8.2 0.9 add_multiply_fusion.diag_ref
  9.4 90.0 %shard_map.46 = bf16[4,128,3456]{2,1,0:T(8,128)(2,1)S(1)} custom-call(s32[2]{0:T(128)S(1)} %pad_add_fusion.bounds_ref, bf16[128,13824]{1,0:T(8,128)(2,1)} %bitcast.49, f32[1,13824]{1,0:T(1,128)S(1)} %add_multiply_fusion.diag_ref, f32[4,13824]{1,0:T(4,128)S(1)} %add_convert_fusion.1.masks_ref), custom_call_target="tpu_custom_call" | custom-call | tf_op jit(solution)/shard_map/pallas_call | solution.py:112
  99.4 1.7 copy-done.2
  101.1 6.3 %all-to-all-start = ((bf16[4,128,3456]{2,1,0:T(8,128)(2,1)}), bf16[4,128,3456]{2,1,0:T(8,128)(2,1)S(1)}, u32[]{:S(2)}, u32[]{:S(2)}) async-start(bf16[4,128,3456]{2,1,0:T(8,128)(2,1)} %copy-done.2), calls=%async_computation | async-start | bytes 7077888 | tf_op jit(solution)/shard_map/all_to_all | solution.py:287
  107.5 1.1 fusion.18
  108.6 1.4 add_convert_fusion.select_ref
  110.2 0.7 add_convert_fusion.2.masks_ref
  110.9 75.6 %all-to-all-done = bf16[4,128,3456]{2,1,0:T(8,128)(2,1)S(1)} async-done(((bf16[4,128,3456]{2,1,0:T(8,128)(2,1)}), bf16[4,128,3456]{2,1,0:T(8,128)(2,1)S(1)}, u32[]{:S(2)}, u32[]{:S(2)}) %all-to-all-start) | async-done | bytes 3538976 | tf_op jit(solution)/shard_map/all_to_all | solution.py:287
  186.5 1.4 fusion.41
  187.9 0.6 copy-done
  188.7 5.2 %shard_map.48 = (bf16[512,384]{1,0:T(8,128)(2,1)S(1)}, bf16[512,384]{1,0:T(8,128)(2,1)}, bf16[512,384]{1,0:T(8,128)(2,1)S(1)}, bf16[512,384]{1,0:T(8,128)(2,1)}) custom-call(bf16[512,3456]{1,0:T(8,128)(2,1)} %bitcast.46, bf16[1152,512]{1,0:T(8,128)(2,1)S(1)} %copy-done.3), custom_call_target="tpu_custom_call" | custom-call | tf_op jit(solution)/shard_map/pallas_call | solution.py:169
  193.9 0.7 copy-done.4
  194.6 0.8 copy-done.6
  195.4 1.1 collective-permute-start.2
  196.5 0.5 collective-permute-start.3
  197.0 1.3 collective-permute-start.1
  198.3 1.3 collective-permute-start
  199.6 0.7 dynamic-slice_add_fusion.diag_ref
  200.4 2.0 copy-done.1
  202.4 39.7 %shard_map.47.inner_ref = f32[512,512]{1,0:T(8,128)S(1)} custom-call(bf16[512,3456]{1,0:T(8,128)(2,1)S(1)} %bitcast.47, bf16[512,3456]{1,0:T(8,128)(2,1)S(1)} %bitcast.48, f32[1,3456]{1,0:T(1,128)S(1)} %dynamic-slice_add_fusion.diag_ref, f32[4,3456]{1,0:T(4,128)S(1)} %copy-done.8), custom_call_target="tpu_custom_call" | custom-call | tf_op jit(solution)/shard_map/pallas_call | solution.py:207
  242.2 0.8 copy-done.13
  243.0 2.7 concatenate.12.far_ref
  245.8 2.9 concatenate.11.near_ref
  248.7 1.0 copy-done.5
  249.7 1.0 copy-done.7
  250.7 4.9 %shard_map.49 = bf16[3,512,512]{2,1,0:T(8,128)(2,1)} custom-call(f32[512,512]{1,0:T(8,128)S(1)} %shard_map.47.inner_ref, bf16[512,1152]{1,0:T(8,128)(2,1)S(1)} %concatenate.11.near_ref, bf16[512,1152]{1,0:T(8,128)(2,1)S(1)} %concatenate.12.far_ref, bf16[512,384]{1,0:T(8,128)(2,1)S(1)} %copy-done.5, bf16[512,384]{1,0:T(8,128)(2,1)} %collective-permute-done.2.rz_ref, ...), custom_call_target="tpu_custom_call" | custom-call | tf_op jit(solution)/shard_map/pallas_call | solution.py:248
  255.7 0.9 copy-done.14
  256.7 2.5 collective-permute-start.4
  259.2 1.5 collective-permute-start.7
  260.7 65.5 %all-reduce.2.cloned.1.call-done = bf16[3,512,512]{2,1,0:T(8,128)(2,1)} async-done(((bf16[3,512,512]{2,1,0:T(8,128)(2,1)}), bf16[3,512,512]{2,1,0:T(8,128)(2,1)}) %all-reduce.2.cloned.1.call-update) | async-done | bytes 1572880 | tf_op jit(solution)/shard_map/psum | solution.py:278
  326.3 1.4 slice_bitcast_fusion.1
  327.9 1.5 collective-permute-start.8
  330.4 17.7 %collective-permute-done.8 = bf16[512,512]{1,0:T(8,128)(2,1)S(1)} collective-permute-done((bf16[512,512]{1,0:T(8,128)(2,1)S(1)}, bf16[512,512]{1,0:T(8,128)(2,1)S(1)}, u32[]{:S(2)}, u32[]{:S(2)}) %collective-permute-start.8) | collective-permute-done | bytes 524320 | tf_op jit(solution)/shard_map/ppermute | solution.py:28
  348.0 0.3 fusion.42
  348.4 0.4 fusion.15
  348.8 1.5 collective-permute-start.11
  350.5 0.8 collective-permute-done.9
  351.9 4.2 %collective-permute-done.11 = bf16[512,128]{1,0:T(8,128)(2,1)S(1)} collective-permute-done((bf16[512,128]{1,0:T(8,128)(2,1)S(1)}, bf16[512,128]{1,0:T(8,128)(2,1)S(1)}, u32[]{:S(2)}, u32[]{:S(2)}) %collective-permute-start.11) | collective-permute-done | bytes 131104 | tf_op jit(solution)/shard_map/ppermute | solution.py:28
  356.8 0.4 fusion.14
  357.2 1.5 collective-permute-start.14
  358.7 2.6 collective-permute-start.12
  361.3 0.8 collective-permute-done.14
  362.2 0.3 fusion.44
  362.5 1.3 collective-permute-done.12
  364.8 0.4 multiply_reduce_fusion
  365.2 0.7 fusion.20
  (58 shorter events, 4.6 us)
Async XLA Ops:
  99.4 1.7 copy-start.2
  101.1 85.4 %all-to-all-start = ((bf16[4,128,3456]{2,1,0:T(8,128)(2,1)}), bf16[4,128,3456]{2,1,0:T(8,128)(2,1)S(1)}, u32[]{:S(2)}, u32[]{:S(2)}) async-start(bf16[4,128,3456]{2,1,0:T(8,128)(2,1)} %copy-done.2), calls=%async_computation | async-start | bytes 7077888 | tf_op jit(solution)/shard_map/all_to_all | solution.py:287
  107.4 218.8 %all-reduce.2.cloned.1.call-start = ((), (), s32[]{:S(2)}) async-start(), calls=%async_computation.1 | async-start | bytes 3145728 | tf_op jit(solution)/shard_map/psum | solution.py:278
  186.5 2.0 copy-start
  186.5 2.1 copy-start.3
  188.7 11.7 %copy-start.8 = (f32[4,3456]{1,0:T(4,128)S(1)}, f32[4,3456]{1,0:T(4,128)}, u32[]{:S(2)}) copy-start(f32[4,3456]{1,0:T(4,128)} %add_convert_fusion.2.masks_ref) | copy-start | bytes 165892
  193.9 0.7 copy-start.4
  194.6 0.8 copy-start.6
  195.4 53.3 %collective-permute-start.2 = (bf16[512,384]{1,0:T(8,128)(2,1)}, bf16[512,384]{1,0:T(8,128)(2,1)}, u32[]{:S(2)}, u32[]{:S(2)}) collective-permute-start(bf16[512,384]{1,0:T(8,128)(2,1)} %get-tuple-element.10), channel_id=1, source_target_pairs={{0,28},{4,0},{8,4},{12,8},{16,12},{20,16},{24,20},{28,24},{1,29},{... | collective-permute-start | bytes 1179656 | tf_op jit(solution)/shard_map/ppermute | solution.py:28
  196.5 52.2 %collective-permute-start.3 = (bf16[512,384]{1,0:T(8,128)(2,1)}, bf16[512,384]{1,0:T(8,128)(2,1)}, u32[]{:S(2)}, u32[]{:S(2)}) collective-permute-start(bf16[512,384]{1,0:T(8,128)(2,1)} %get-tuple-element.12), channel_id=1, source_target_pairs={{0,16},{4,20},{8,24},{12,28},{16,0},{20,4},{24,8},{28,12},{1,17},{... | collective-permute-start | bytes 1179656 | tf_op jit(solution)/shard_map/ppermute | solution.py:28
  197.0 45.1 %collective-permute-start.1 = (bf16[512,288]{1,0:T(8,128)(2,1)S(1)}, bf16[512,288]{1,0:T(8,128)(2,1)S(1)}, u32[]{:S(2)}, u32[]{:S(2)}) collective-permute-start(bf16[512,288]{1,0:T(8,128)(2,1)S(1)} %get-tuple-element.13), channel_id=1, source_target_pairs={{0,1},{1,2},{2,3},{4,5},{5,6},{6,7},{8,9},{9,10},{10,11},{12,13},{... | collective-permute-start | bytes 884744 | tf_op jit(solution)/shard_map/ppermute | solution.py:298
  198.3 43.8 %collective-permute-start = (bf16[512,288]{1,0:T(8,128)(2,1)S(1)}, bf16[512,288]{1,0:T(8,128)(2,1)S(1)}, u32[]{:S(2)}, u32[]{:S(2)}) collective-permute-start(bf16[512,288]{1,0:T(8,128)(2,1)S(1)} %get-tuple-element.15), channel_id=1, source_target_pairs={{1,0},{2,1},{3,2},{5,4},{6,5},{7,6},{9,8},{10,9},{11,10},{13,12},{... | collective-permute-start | bytes 884744 | tf_op jit(solution)/shard_map/ppermute | solution.py:297
  200.4 2.0 copy-start.1
  202.4 40.7 %copy-start.10 = (bf16[512,288]{1,0:T(8,128)(2,1)S(1)}, bf16[512,288]{1,0:T(8,128)(2,1)}, u32[]{:S(2)}) copy-start(bf16[512,288]{1,0:T(8,128)(2,1)} %get-tuple-element.14) | copy-start | bytes 884740
  202.4 40.7 %copy-start.11 = (bf16[512,288]{1,0:T(8,128)(2,1)S(1)}, bf16[512,288]{1,0:T(8,128)(2,1)}, u32[]{:S(2)}) copy-start(bf16[512,288]{1,0:T(8,128)(2,1)} %get-tuple-element.16) | copy-start | bytes 884740
  242.1 0.9 copy-start.12
  242.1 0.8 copy-start.13
  248.7 1.0 copy-start.5
  249.7 1.0 copy-start.7
  255.6 0.9 copy-start.14
  256.6 91.8 %collective-permute-start.6 = (bf16[512,128]{1,0:T(8,128)(2,1)S(1)}, bf16[512,128]{1,0:T(8,128)(2,1)S(1)}, u32[]{:S(2)}, u32[]{:S(2)}) collective-permute-start(bf16[512,128]{1,0:T(8,128)(2,1)S(1)} %bitcast.50), channel_id=1, source_target_pairs={{0,4},{4,8},{8,12},{12,16},{16,20},{20,24},{24,28},{28,0},{1,5},{5... | collective-permute-start | bytes 393224 | tf_op jit(solution)/shard_map/ppermute | solution.py:28
  256.7 72.7 %collective-permute-start.4 = (bf16[512,128]{1,0:T(8,128)(2,1)S(1)}, bf16[512,128]{1,0:T(8,128)(2,1)S(1)}, u32[]{:S(2)}, u32[]{:S(2)}) collective-permute-start(bf16[512,128]{1,0:T(8,128)(2,1)S(1)} %bitcast.51), channel_id=1, source_target_pairs={{0,28},{4,0},{8,4},{12,8},{16,12},{20,16},{24,20},{28,24},{1,29},{... | collective-permute-start | bytes 393224 | tf_op jit(solution)/shard_map/ppermute | solution.py:28
  259.2 70.5 %collective-permute-start.7 = (bf16[512,128]{1,0:T(8,128)(2,1)S(1)}, bf16[512,128]{1,0:T(8,128)(2,1)S(1)}, u32[]{:S(2)}, u32[]{:S(2)}) collective-permute-start(bf16[512,128]{1,0:T(8,128)(2,1)S(1)} %bitcast.52), channel_id=1, source_target_pairs={{0,16},{4,20},{8,24},{12,28},{16,0},{20,4},{24,8},{28,12},{1,17},{... | collective-permute-start | bytes 393224 | tf_op jit(solution)/shard_map/ppermute | solution.py:28
  326.3 3.2 copy-start.9
  327.7 20.7 %collective-permute-start.5 = (bf16[512,512]{1,0:T(8,128)(2,1)S(1)}, bf16[512,512]{1,0:T(8,128)(2,1)S(1)}, u32[]{:S(2)}, u32[]{:S(2)}) collective-permute-start(bf16[512,512]{1,0:T(8,128)(2,1)S(1)} %get-tuple-element.17), channel_id=1, source_target_pairs={{0,4},{4,8},{8,12},{12,16},{16,20},{20,24},{24,28},{28,0},{1,5},{5... | collective-permute-start | bytes 1572872 | tf_op jit(solution)/shard_map/ppermute | solution.py:28
  327.9 20.1 %collective-permute-start.8 = (bf16[512,512]{1,0:T(8,128)(2,1)S(1)}, bf16[512,512]{1,0:T(8,128)(2,1)S(1)}, u32[]{:S(2)}, u32[]{:S(2)}) collective-permute-start(bf16[512,512]{1,0:T(8,128)(2,1)S(1)} %get-tuple-element.18), channel_id=1, source_target_pairs={{0,16},{4,20},{8,24},{12,28},{16,0},{20,4},{24,8},{28,12},{1,17},{... | collective-permute-start | bytes 1572872 | tf_op jit(solution)/shard_map/ppermute | solution.py:28
  348.8 2.6 collective-permute-start.9
  348.8 7.3 %collective-permute-start.11 = (bf16[512,128]{1,0:T(8,128)(2,1)S(1)}, bf16[512,128]{1,0:T(8,128)(2,1)S(1)}, u32[]{:S(2)}, u32[]{:S(2)}) collective-permute-start(bf16[512,128]{1,0:T(8,128)(2,1)S(1)} %fusion.15), channel_id=1, source_target_pairs={{0,16},{4,20},{8,24},{12,28},{16,0},{20,4},{24,8},{28,12},{1,17},{... | collective-permute-start | bytes 393224 | tf_op jit(solution)/shard_map/ppermute | solution.py:28
  350.4 6.4 %collective-permute-start.10 = (bf16[512,128]{1,0:T(8,128)(2,1)S(1)}, bf16[512,128]{1,0:T(8,128)(2,1)S(1)}, u32[]{:S(2)}, u32[]{:S(2)}) collective-permute-start(bf16[512,128]{1,0:T(8,128)(2,1)S(1)} %fusion.15), channel_id=1, source_target_pairs={{0,4},{4,8},{8,12},{12,16},{16,20},{20,24},{24,28},{28,0},{1,5},{5... | collective-permute-start | bytes 393224 | tf_op jit(solution)/shard_map/ppermute | solution.py:28
  357.2 5.0 %collective-permute-start.14 = (bf16[512,128]{1,0:T(8,128)(2,1)S(1)}, bf16[512,128]{1,0:T(8,128)(2,1)S(1)}, u32[]{:S(2)}, u32[]{:S(2)}) collective-permute-start(bf16[512,128]{1,0:T(8,128)(2,1)S(1)} %fusion.14), channel_id=1, source_target_pairs={{0,16},{4,20},{8,24},{12,28},{16,0},{20,4},{24,8},{28,12},{1,17},{... | collective-permute-start | bytes 393224 | tf_op jit(solution)/shard_map/ppermute | solution.py:28
  358.7 6.1 %collective-permute-start.13 = (bf16[512,128]{1,0:T(8,128)(2,1)S(1)}, bf16[512,128]{1,0:T(8,128)(2,1)S(1)}, u32[]{:S(2)}, u32[]{:S(2)}) collective-permute-start(bf16[512,128]{1,0:T(8,128)(2,1)S(1)} %fusion.14), channel_id=1, source_target_pairs={{0,4},{4,8},{8,12},{12,16},{16,20},{20,24},{24,28},{28,0},{1,5},{5... | collective-permute-start | bytes 393224 | tf_op jit(solution)/shard_map/ppermute | solution.py:28
  358.7 5.2 %collective-permute-start.12 = (bf16[512,128]{1,0:T(8,128)(2,1)S(1)}, bf16[512,128]{1,0:T(8,128)(2,1)S(1)}, u32[]{:S(2)}, u32[]{:S(2)}) collective-permute-start(bf16[512,128]{1,0:T(8,128)(2,1)S(1)} %fusion.14), channel_id=1, source_target_pairs={{0,28},{4,0},{8,4},{12,8},{16,12},{20,16},{24,20},{28,24},{1,29},{... | collective-permute-start | bytes 393224 | tf_op jit(solution)/shard_map/ppermute | solution.py:28
Sparse Core Ops, SparseCore 0:
  255.8 70.4 all-reduce.1

commit v2 on v1

v2 whole, which is shorter than its diff:
```python
import functools

import jax
import jax.numpy as jnp
from jax import lax
from jax.experimental import pallas as pl
from jax.experimental.pallas import tpu as pltpu
from jax.sharding import PartitionSpec as P
import ml_dtypes
import numpy as np

P_SIZE = 24
G = 13824
EB = 4
PLANE = P_SIZE * P_SIZE
PAD = 640
TILE = 256
PERIOD = 9
SPANS = ((-640, -256), (-128, 384), (512, 896))


LOW_EDGE = 4.0
HIGH_EDGE = 14.0
SHIFT_CENTER = 4.0
HALF_WIDTH = 6.0
VMEM_LIMIT = 48 * 1024 * 1024
NT = (((1,), (1,)), ((), ()))


def from_behind(value, axis, by):
    devices = lax.axis_size(axis)
    return lax.ppermute(value, axis, [(i, (i + by) % devices) for i in range(devices)])


def stencil_tables():
    tables = []
    source = np.concatenate([np.arange(*span) for span in SPANS])[:, None]
    for which in range(PERIOD):
        column = np.arange(TILE)[None]
        zpos = (which * TILE + column) % P_SIZE
        ypos = (which * TILE + column) // P_SIZE % P_SIZE
        hit = (source == column + PLANE) | (source == column - PLANE)
        hit = hit | ((source == column + 1) & (zpos < P_SIZE - 1))
        hit = hit | ((source == column - 1) & (zpos > 0))
        hit = hit | ((source == column + P_SIZE) & (ypos < P_SIZE - 1))
        hit = hit | ((source == column - P_SIZE) & (ypos > 0))
        tables.append(hit)
    return jnp.asarray(np.stack(tables).astype(ml_dtypes.bfloat16))


def padded_width(length):
    return 2 * PAD + (length + TILE - 1) // TILE * TILE


def windows(ref, at):
    parts = []
    for low, high in SPANS:
        start = PAD + at + low
        if not isinstance(at, int):
            start = pl.multiple_of(start, 128)
        parts.append(ref[:, pl.ds(start, high - low)])
    return jnp.concatenate(parts, axis=1)


def clear_pads(ref, length):
    ref[:, 0:PAD] = jnp.zeros((ref.shape[0], PAD), ref.dtype)
    inner = PAD + length // 128 * 128
    ref[:, inner:] = jnp.zeros((ref.shape[0], ref.shape[1] - inner), ref.dtype)


def filter_kernel(slabs, bounds_ref, orbitals_ref, diag_ref, table_ref, out_ref, low_ref, mid_ref, wide_ref):
    spread = 0.5 * (HIGH_EDGE - LOW_EDGE)
    rows, length = orbitals_ref.shape
    turn = PERIOD * TILE
    repeats = length // turn
    clear_pads(low_ref, length)
    clear_pads(mid_ref, length)
    low_ref[:, PAD : PAD + length] = orbitals_ref[...]

    def sums(ref, which):
        offset = which * TILE
        left = jnp.concatenate([windows(ref, offset + turn * r) for r in range(repeats)], axis=0)
        return jnp.dot(left, table_ref[which], preferred_element_type=jnp.float32)

    def tile_at(which, r):
        return pl.multiple_of(which * TILE + turn * r, TILE)

    @pl.loop(0, PERIOD)
    def _(which):
        total = sums(low_ref, which)
        for r in range(repeats):
            at = tile_at(which, r)
            value = diag_ref[0:1, pl.ds(at, TILE)] * orbitals_ref[:, pl.ds(at, TILE)].astype(
                jnp.float32
            ) - total[r * rows : (r + 1) * rows] * (1.0 / spread)
            wide_ref[:, pl.ds(at, TILE)] = value
            mid_ref[:, pl.ds(pl.multiple_of(PAD + at, 128), TILE)] = value.astype(jnp.bfloat16)

    def second(which, squares):
        total = sums(mid_ref, which)
        for r in range(repeats):
            at = tile_at(which, r)
            value = (
                2.0 * diag_ref[0:1, pl.ds(at, TILE)] * wide_ref[:, pl.ds(at, TILE)]
                - total[r * rows : (r + 1) * rows] * (2.0 / spread)
                - orbitals_ref[:, pl.ds(at, TILE)].astype(jnp.float32)
            )
            wide_ref[:, pl.ds(at, TILE)] = value
            squares = squares + value * value
        return squares

    squares = lax.fori_loop(0, PERIOD, second, jnp.zeros((rows, TILE), jnp.float32))
    squares = jnp.sum(squares, axis=1, keepdims=True)
    scale = 1.0 / jnp.sqrt(squares * (1.0 / length) + 1e-06)
    row = bounds_ref[1] + lax.broadcasted_iota(jnp.int32, (rows, 1), 0)
    scale = jnp.where(row < bounds_ref[0], scale, 0.0)
    share = length // slabs
    for slab in range(slabs):
        out_ref[slab] = (wide_ref[:, slab * share : (slab + 1) * share] * scale).astype(jnp.bfloat16)


def filtered_basis(orbitals, potential, kept_count, start_index, slabs, table):
    count, length = orbitals.shape
    middle = 0.5 * (HIGH_EDGE + LOW_EDGE)
    spread = 0.5 * (HIGH_EDGE - LOW_EDGE)
    diag = ((6.0 - middle) + potential)[None] / spread
    bounds = jnp.stack([kept_count, start_index]).astype(jnp.int32)
    whole = pl.BlockSpec(memory_space=pltpu.VMEM)
    return pl.pallas_call(
        functools.partial(filter_kernel, slabs),
        in_specs=[pl.BlockSpec(memory_space=pltpu.SMEM), whole, whole, whole],
        out_specs=whole,
        out_shape=jax.ShapeDtypeStruct((slabs, count, length // slabs), jnp.bfloat16),
        scratch_shapes=[
            pltpu.VMEM((count, padded_width(length)), jnp.bfloat16),
            pltpu.VMEM((count, padded_width(length)), jnp.bfloat16),
            pltpu.VMEM((count, length), jnp.float32),
        ],
        compiler_params=pltpu.CompilerParams(vmem_limit_bytes=VMEM_LIMIT),
    )(bounds, orbitals, diag, table)


def face_chunk(length):
    return 1152 if length % 1152 == 0 else length


def face_selector(chunk):
    points = chunk // P_SIZE
    group = (2 * points + 127) // 128 * 128
    where = np.arange(chunk)[:, None]
    zpos, ypos, xpos = where % P_SIZE, where // P_SIZE % P_SIZE, where // PLANE
    column = np.arange(group)[None]
    point, late = column % points, column >= points
    used = column < 2 * points
    top = P_SIZE - 1
    layers = [(top - 1, top), (0, 1)]
    parts = []
    for pos, spot in ((zpos, where // P_SIZE), (ypos, xpos * P_SIZE + zpos)):
        for early_layer, late_layer in layers:
            layer = np.where(late, late_layer, early_layer)
            parts.append(((spot == point) & (pos == layer) & used))
    return jnp.asarray(np.concatenate(parts, axis=1).astype(ml_dtypes.bfloat16))


def faces_kernel(rows_ref, select_ref, lz_ref, rz_ref, ly_ref, ry_ref):
    chunk = select_ref.shape[0]
    group = select_ref.shape[1] // 4
    for which in range(rows_ref.shape[1] // chunk):
        picked = jnp.dot(
            rows_ref[:, which * chunk : (which + 1) * chunk],
            select_ref[...],
            preferred_element_type=jnp.float32,
        ).astype(jnp.bfloat16)
        for place, out in enumerate((lz_ref, rz_ref, ly_ref, ry_ref)):
            out[:, which * group : (which + 1) * group] = picked[:, place * group : (place + 1) * group]


def face_layers(rows):
    count, length = rows.shape
    chunk = face_chunk(length)
    select = face_selector(chunk)
    width = length // chunk * (select.shape[1] // 4)
    step = count // 4
    return pl.pallas_call(
        faces_kernel,
        grid=(4,),
        in_specs=[
            pl.BlockSpec((step, length), lambda i: (i, 0)),
            pl.BlockSpec(select.shape, lambda i: (0, 0)),
        ],
        out_specs=[pl.BlockSpec((step, width), lambda i: (i, 0))] * 4,
        out_shape=[jax.ShapeDtypeStruct((count, width), jnp.bfloat16)] * 4,
        compiler_params=pltpu.CompilerParams(vmem_limit_bytes=VMEM_LIMIT),
    )(rows, select)


def interior_kernel(all_ref, rows_ref, diag_ref, table_ref, out_ref, wide_ref, applied_ref):
    count, length = rows_ref.shape
    clear_pads(wide_ref, length)
    wide_ref[:, PAD : PAD + length] = rows_ref[...]
    for at in range(0, length, TILE):
        size = min(TILE, length - at)
        total = jnp.dot(
            windows(wide_ref, at), table_ref[at // TILE % PERIOD], preferred_element_type=jnp.float32
        )
        applied_ref[:, at : at + size] = (
            diag_ref[0:1, at : at + size] * rows_ref[:, at : at + size].astype(jnp.float32)
            - total[:, :size]
        ).astype(jnp.bfloat16)
    out_ref[...] = lax.dot_general(
        applied_ref[...], all_ref[...], NT, preferred_element_type=jnp.float32
    )


def interior_block(rows, slab_potential, table):
    count, length = rows.shape
    step = count // 2
    return pl.pallas_call(
        interior_kernel,
        grid=(2,),
        in_specs=[
            pl.BlockSpec((count, length), lambda i: (0, 0)),
            pl.BlockSpec((step, length), lambda i: (i, 0)),
            pl.BlockSpec((1, length), lambda i: (0, 0)),
            pl.BlockSpec(table.shape, lambda i: (0, 0, 0)),
        ],
        out_specs=pl.BlockSpec((step, count), lambda i: (i, 0)),
        out_shape=jax.ShapeDtypeStruct((count, count), jnp.float32),
        scratch_shapes=[
            pltpu.VMEM((step, padded_width(length)), jnp.bfloat16),
            pltpu.VMEM((step, length), jnp.bfloat16),
        ],
        compiler_params=pltpu.CompilerParams(vmem_limit_bytes=VMEM_LIMIT),
    )(rows, rows, (6.0 + slab_potential)[None], table)


def partials_kernel(inner_ref, near_ref, far_ref, lz_ref, rz_ref, ly_ref, ry_ref, out_ref):
    def product(a, b):
        return lax.dot_general(a, b, NT, preferred_element_type=jnp.float32)

    seam = product(near_ref[...], far_ref[...])
    out_ref[0] = ((inner_ref[...] - seam) * (1.0 / G)).astype(jnp.bfloat16)
    weight = -0.5 / PLANE
    out_ref[1] = (product(lz_ref[...], rz_ref[...]) * weight).astype(jnp.bfloat16)
    out_ref[2] = (product(ly_ref[...], ry_ref[...]) * weight).astype(jnp.bfloat16)


def partial_blocks(inner, near, far, lz, rz, ly, ry):
    count = inner.shape[0]
    step = count // 4

    def cut(value):
        return pl.BlockSpec((step, value.shape[1]), lambda i: (i, 0))

    def full(value):
        return pl.BlockSpec(value.shape, lambda i: (0, 0))

    return pl.pallas_call(
        partials_kernel,
        grid=(4,),
        in_specs=[cut(inner), cut(near), full(far), cut(lz), full(rz), cut(ly), full(ry)],
        out_specs=pl.BlockSpec((3, step, count), lambda i: (0, i, 0)),
        out_shape=jax.ShapeDtypeStruct((3, count, count), jnp.bfloat16),
        compiler_params=pltpu.CompilerParams(vmem_limit_bytes=VMEM_LIMIT),
    )(inner, near, far, lz, rz, ly, ry)


def apply_blocks(terms, current):
    offsets = [0, 1, -1, EB, -EB]
    running = jnp.zeros((terms[0][0].shape[0], current.shape[1]), jnp.float32)
    for position, offset in enumerate(offsets):
        matrix, contract = terms[position]
        if offset == 0:
            source = current
        else:
            source = from_behind(current, "elem", -offset)
        running = running + lax.dot_general(
            matrix, source, (((contract,), (0,)), ((), ())), preferred_element_type=jnp.float32
        )
    return running


def scaled(terms, current):
    return (apply_blocks(terms, current) - SHIFT_CENTER * current.astype(jnp.float32)) / HALF_WIDTH


def summed_blocks(partials):
    return lax.psum(partials, "band")


def on_device(orbitals, potential, basis_count, states):
    per_device = orbitals.shape[1]
    slabs = lax.axis_size("band")
    band_place = lax.axis_index("band")
    table = stencil_tables()
    start_index = band_place * per_device
    basis = filtered_basis(orbitals[0], potential[0], basis_count[0], start_index, slabs, table)
    basis_rows = lax.all_to_all(basis, "band", split_axis=0, concat_axis=0, tiled=True)
    basis_rows = basis_rows.reshape(slabs * per_device, -1)
    slab_length = basis_rows.shape[1]
    slab_potential = lax.dynamic_slice_in_dim(
        potential[0], band_place * slab_length, slab_length, 0
    )
    half = PLANE // 2
    initial, last = basis_rows[:, :PLANE], basis_rows[:, slab_length - PLANE :]
    up = [(i, i + 1) for i in range(slabs - 1)]
    down = [(j, i) for i, j in up]
    after = lax.ppermute(initial[:, :half], "band", down)
    before = lax.ppermute(last[:, half:], "band", up)
    lz, rz, ly, ry = face_layers(basis_rows)
    rz = from_behind(rz, "elem", -1)
    ry = from_behind(ry, "elem", -EB)
    inner = interior_block(basis_rows, slab_potential, table)
    near = jnp.concatenate([last[:, :half], after, initial[:, half:], before], axis=1)
    far = jnp.concatenate([after, last[:, :half], before, initial[:, half:]], axis=1)
    partials = partial_blocks(inner, near, far, lz, rz, ly, ry)
    summed = summed_blocks(partials)
    mirrored = []
    for position, offset in ((1, 1), (2, EB)):
        mirrored.append(from_behind(summed[position], "elem", offset))
    terms = [(summed[0], 1), (summed[1], 1), (mirrored[0], 0), (summed[2], 1), (mirrored[1], 0)]
    start_states = states[0]
    first_term = scaled(terms, start_states).astype(jnp.bfloat16)
    second_term = (2.0 * scaled(terms, first_term) - start_states.astype(jnp.float32)).astype(
        jnp.bfloat16
    )
    third_term = 2.0 * scaled(terms, second_term) - first_term.astype(jnp.float32)
    magnitude = jnp.sqrt(jnp.mean(third_term * third_term, axis=0, keepdims=True) + 1e-06)
    return (third_term / magnitude).astype(jnp.bfloat16)[None]


def solution(mesh):
    placed = (P("elem", "band", None), P("elem", None), P("elem"), P("elem", None, "band"))
    return jax.shard_map(
        on_device, mesh=mesh, in_specs=placed, out_specs=P("elem", None, "band"), check_vma=False
    )
```

time: 373 us -> 270 us (0.72)
  Pallas kernels: 140 us -> 37.7 us
  other arithmetic: 7.08 us -> 2.39 us
  waiting for transfers between devices: 166 us -> 170 us
    pallas_call x2, Pallas kernels: 130 us -> 27.5 us  [the longest x1 17.7 us: filtered_basis(): pl.pallas_call(functools.partial(filter_kernel, slabs), in_specs=[pl.Bloc...]
    unnamed x30 -> x28, local copies, waits for them, and re-layouts: 9.75 us -> 9.76 us
  transfers between devices with their start and end apart: 17 -> 17, of which waited for: 7 -> 7; matrix products, arithmetic and copies ran while one was open for 4% -> 4% of each run, Pallas kernels for 11% -> 4%
where the time goes in v2:
time: 270 us; the launch traced here: 269 us
  waiting for transfers between devices  170 us (63%)
  Pallas kernels  37.7 us (14%)
  starting transfers between devices  22.3 us (8%)
  local copies, waits for them, and re-layouts  18.2 us (7%)
  between operations  14.3 us (5%)
  matrix products  4.73 us (2%)
    all_to_all x1, waiting for transfers between devices, on_device(): lax.all_to_all(basis, 'band', split_axis=0, concat_axis=0, tiled=True)  79.1 us
    psum x1, waiting for transfers between devices, summed_blocks(): return lax.psum(partials, 'band')  65.6 us
    ppermute x13, waiting for transfers between devices, from_behind(): lax.ppermute(value, axis, [(i, (i + by) % devices) for i in range(devices)])  24.9 us
    pallas_call x1, Pallas kernels, filtered_basis(): pl.pallas_call(functools.partial(filter_kernel, slabs), in_specs=[pl.Bloc...  17.7 us
    ppermute x13, starting transfers between devices, from_behind(): lax.ppermute(value, axis, [(i, (i + by) % devices) for i in range(devices)])  13.4 us
    unnamed x28, local copies, waits for them, and re-layouts  9.76 us
    pallas_call x1, Pallas kernels, interior_block(): pl.pallas_call(interior_kernel, grid=(2,), in_specs=[pl.BlockSpec((count,...  9.76 us
    all_to_all x1, starting transfers between devices, on_device(): lax.all_to_all(basis, 'band', split_axis=0, concat_axis=0, tiled=True)  6.32 us
  transfers between devices with their start and end apart: 17, of which 7 were waited for; matrix products, arithmetic and copies ran while one was open for 4% of the time, Pallas kernels for 4%

profile of v2, /device:TPU:0, one launch (start us, length us, event | category | flops | bytes accessed | tf_op | source)
XLA Modules:
  0.0 269.2 jit_solution(12920612661425652249)
XLA Ops:
  7.2 0.9 add_multiply_fusion.diag_ref
  8.2 17.7 %shard_map.64 = bf16[4,128,3456]{2,1,0:T(8,128)(2,1)S(1)} custom-call(s32[2]{0:T(128)S(1)} %pad_add_fusion.bounds_ref, bf16[128,13824]{1,0:T(8,128)(2,1)} %bitcast.49, f32[1,13824]{1,0:T(1,128)S(1)} %add_multiply_fusion.diag_ref, bf16[9,1280,256]{2,1,0:T(8,128)(2,1)} %constant.42.clone.table_ref), custom_call_target="tpu_custom_call" | custom-call | tf_op jit(solution)/shard_map/pallas_call | solution.py:129
  25.9 1.7 copy-done.2
  27.6 6.3 %all-to-all-start = ((bf16[4,128,3456]{2,1,0:T(8,128)(2,1)}), bf16[4,128,3456]{2,1,0:T(8,128)(2,1)S(1)}, u32[]{:S(2)}, u32[]{:S(2)}) async-start(bf16[4,128,3456]{2,1,0:T(8,128)(2,1)} %copy-done.2), calls=%async_computation | async-start | bytes 7077888 | tf_op jit(solution)/shard_map/all_to_all | solution.py:298
  33.9 79.1 %all-to-all-done = bf16[4,128,3456]{2,1,0:T(8,128)(2,1)S(1)} async-done(((bf16[4,128,3456]{2,1,0:T(8,128)(2,1)}), bf16[4,128,3456]{2,1,0:T(8,128)(2,1)S(1)}, u32[]{:S(2)}, u32[]{:S(2)}) %all-to-all-start) | async-done | bytes 3538976 | tf_op jit(solution)/shard_map/all_to_all | solution.py:298
  113.0 1.4 fusion.24
  114.4 0.6 copy-done
  115.1 5.3 %shard_map.66 = (bf16[512,384]{1,0:T(8,128)(2,1)S(1)}, bf16[512,384]{1,0:T(8,128)(2,1)}, bf16[512,384]{1,0:T(8,128)(2,1)S(1)}, bf16[512,384]{1,0:T(8,128)(2,1)}) custom-call(bf16[512,3456]{1,0:T(8,128)(2,1)} %bitcast.46, bf16[1152,512]{1,0:T(8,128)(2,1)S(1)} %copy-done.3), custom_call_target="tpu_custom_call" | custom-call | tf_op jit(solution)/shard_map/pallas_call | solution.py:184
  120.4 0.8 copy-done.4
  121.2 0.7 copy-done.6
  121.9 1.3 collective-permute-start.1
  123.2 1.3 collective-permute-start
  124.5 1.2 collective-permute-start.2
  125.7 0.5 collective-permute-start.3
  126.2 0.7 dynamic-slice_add_fusion.diag_ref
  126.9 2.0 copy-done.1
  128.9 9.8 %shard_map.65.inner_ref = f32[512,512]{1,0:T(8,128)S(1)} custom-call(bf16[512,3456]{1,0:T(8,128)(2,1)S(1)} %bitcast.47, bf16[512,3456]{1,0:T(8,128)(2,1)S(1)} %bitcast.48, f32[1,3456]{1,0:T(1,128)S(1)} %dynamic-slice_add_fusion.diag_ref, bf16[9,1280,256]{2,1,0:T(8,128)(2,1)} %constant.42.clone.table_ref), custom_call_target="tpu_custom_call" | custom-call | tf_op jit(solution)/shard_map/pallas_call | solution.py:218
  138.7 0.8 copy-done.12
  139.6 2.7 %concatenate.7.far_ref = bf16[512,1152]{1,0:T(8,128)(2,1)S(1)} concatenate(bf16[512,288]{1,0:T(8,128)(2,1)} %copy-done.12, bf16[512,288]{1,0:T(8,128)(2,1)S(1)} %copy-done.10, bf16[512,288]{1,0:T(8,128)(2,1)S(1)} %collective-permute-done.1, bf16[512,288]{1,0:T(8,128)(2,1)S(1)} %copy-done.9), dimensions={1} | concatenate | bytes 2359296 | tf_op jit(solution)/shard_map/concatenate | solution.py:315
  142.3 2.9 %concatenate.6.near_ref = bf16[512,1152]{1,0:T(8,128)(2,1)S(1)} concatenate(bf16[512,288]{1,0:T(8,128)(2,1)} %get-tuple-element.16, bf16[512,288]{1,0:T(8,128)(2,1)} %copy-done.12, bf16[512,288]{1,0:T(8,128)(2,1)} %get-tuple-element.14, bf16[512,288]{1,0:T(8,128)(2,1)} %copy-done.11), dimensions={1} | concatenate | bytes 2359296 | tf_op jit(solution)/shard_map/concatenate | solution.py:314
  145.3 1.0 copy-done.5
  146.3 1.0 copy-done.7
  147.3 5.0 %shard_map.67 = bf16[3,512,512]{2,1,0:T(8,128)(2,1)} custom-call(f32[512,512]{1,0:T(8,128)S(1)} %shard_map.65.inner_ref, bf16[512,1152]{1,0:T(8,128)(2,1)S(1)} %concatenate.6.near_ref, bf16[512,1152]{1,0:T(8,128)(2,1)S(1)} %concatenate.7.far_ref, bf16[512,384]{1,0:T(8,128)(2,1)S(1)} %copy-done.5, bf16[512,384]{1,0:T(8,128)(2,1)} %collective-permute-done.2.rz_ref, ...), custom_call_target="tpu_custom_call" | custom-call | tf_op jit(solution)/shard_map/pallas_call | solution.py:258
  152.3 0.9 copy-done.13
  153.3 2.5 collective-permute-start.4
  155.8 1.5 collective-permute-start.7
  157.3 65.6 %all-reduce.2.cloned.1.call-done = bf16[3,512,512]{2,1,0:T(8,128)(2,1)} async-done(((bf16[3,512,512]{2,1,0:T(8,128)(2,1)}), bf16[3,512,512]{2,1,0:T(8,128)(2,1)}) %all-reduce.2.cloned.1.call-update) | async-done | bytes 1572880 | tf_op jit(solution)/shard_map/psum | solution.py:288
  223.0 1.4 slice_bitcast_fusion.1
  224.4 1.5 collective-permute-start.8
  226.0 0.3 fusion.20
  226.3 0.3 fusion.23
  226.9 17.7 %collective-permute-done.8 = bf16[512,512]{1,0:T(8,128)(2,1)S(1)} collective-permute-done((bf16[512,512]{1,0:T(8,128)(2,1)S(1)}, bf16[512,512]{1,0:T(8,128)(2,1)S(1)}, u32[]{:S(2)}, u32[]{:S(2)}) %collective-permute-start.8) | collective-permute-done | bytes 524320 | tf_op jit(solution)/shard_map/ppermute | solution.py:32
  244.6 0.3 fusion.25
  244.9 0.4 fusion.15
  245.3 1.5 collective-permute-start.11
  247.1 0.8 collective-permute-done.9
  248.5 4.2 %collective-permute-done.11 = bf16[512,128]{1,0:T(8,128)(2,1)S(1)} collective-permute-done((bf16[512,128]{1,0:T(8,128)(2,1)S(1)}, bf16[512,128]{1,0:T(8,128)(2,1)S(1)}, u32[]{:S(2)}, u32[]{:S(2)}) %collective-permute-start.11) | collective-permute-done | bytes 131104 | tf_op jit(solution)/shard_map/ppermute | solution.py:32
  252.7 0.3 fusion.26
  253.3 0.4 fusion.14
  253.7 1.5 collective-permute-start.14
  255.2 2.6 collective-permute-start.12
  257.9 0.8 collective-permute-done.14
  258.7 0.3 fusion.27
  259.0 1.3 collective-permute-done.12
  260.7 0.3 convolution_add_fusion.1
  261.0 0.3 fusion.21
  261.3 0.4 multiply_reduce_fusion
  261.7 0.7 fusion.16
  (43 shorter events, 2.3 us)
Async XLA Ops:
  25.9 1.7 copy-start.2
  27.6 85.4 %all-to-all-start = ((bf16[4,128,3456]{2,1,0:T(8,128)(2,1)}), bf16[4,128,3456]{2,1,0:T(8,128)(2,1)S(1)}, u32[]{:S(2)}, u32[]{:S(2)}) async-start(bf16[4,128,3456]{2,1,0:T(8,128)(2,1)} %copy-done.2), calls=%async_computation | async-start | bytes 7077888 | tf_op jit(solution)/shard_map/all_to_all | solution.py:298
  33.9 189.0 %all-reduce.2.cloned.1.call-start = ((), (), s32[]{:S(2)}) async-start(), calls=%async_computation.1 | async-start | bytes 3145728 | tf_op jit(solution)/shard_map/psum | solution.py:288
  113.0 2.0 copy-start
  113.0 2.1 copy-start.3
  120.4 0.8 copy-start.4
  121.2 0.7 copy-start.6
  121.9 16.8 %collective-permute-start.1 = (bf16[512,288]{1,0:T(8,128)(2,1)S(1)}, bf16[512,288]{1,0:T(8,128)(2,1)S(1)}, u32[]{:S(2)}, u32[]{:S(2)}) collective-permute-start(bf16[512,288]{1,0:T(8,128)(2,1)S(1)} %get-tuple-element.13), channel_id=1, source_target_pairs={{0,1},{1,2},{2,3},{4,5},{5,6},{6,7},{8,9},{9,10},{10,11},{12,13},{... | collective-permute-start | bytes 884744 | tf_op jit(solution)/shard_map/ppermute | solution.py:309
  123.2 15.5 %collective-permute-start = (bf16[512,288]{1,0:T(8,128)(2,1)S(1)}, bf16[512,288]{1,0:T(8,128)(2,1)S(1)}, u32[]{:S(2)}, u32[]{:S(2)}) collective-permute-start(bf16[512,288]{1,0:T(8,128)(2,1)S(1)} %get-tuple-element.15), channel_id=1, source_target_pairs={{1,0},{2,1},{3,2},{5,4},{6,5},{7,6},{9,8},{10,9},{11,10},{13,12},{... | collective-permute-start | bytes 884744 | tf_op jit(solution)/shard_map/ppermute | solution.py:308
  124.5 20.8 %collective-permute-start.2 = (bf16[512,384]{1,0:T(8,128)(2,1)}, bf16[512,384]{1,0:T(8,128)(2,1)}, u32[]{:S(2)}, u32[]{:S(2)}) collective-permute-start(bf16[512,384]{1,0:T(8,128)(2,1)} %get-tuple-element.10), channel_id=1, source_target_pairs={{0,28},{4,0},{8,4},{12,8},{16,12},{20,16},{24,20},{28,24},{1,29},{... | collective-permute-start | bytes 1179656 | tf_op jit(solution)/shard_map/ppermute | solution.py:32
  125.7 19.6 %collective-permute-start.3 = (bf16[512,384]{1,0:T(8,128)(2,1)}, bf16[512,384]{1,0:T(8,128)(2,1)}, u32[]{:S(2)}, u32[]{:S(2)}) collective-permute-start(bf16[512,384]{1,0:T(8,128)(2,1)} %get-tuple-element.12), channel_id=1, source_target_pairs={{0,16},{4,20},{8,24},{12,28},{16,0},{20,4},{24,8},{28,12},{1,17},{... | collective-permute-start | bytes 1179656 | tf_op jit(solution)/shard_map/ppermute | solution.py:32
  126.9 2.0 copy-start.1
  128.9 10.7 %copy-start.9 = (bf16[512,288]{1,0:T(8,128)(2,1)S(1)}, bf16[512,288]{1,0:T(8,128)(2,1)}, u32[]{:S(2)}) copy-start(bf16[512,288]{1,0:T(8,128)(2,1)} %get-tuple-element.14) | copy-start | bytes 884740
  128.9 10.7 %copy-start.10 = (bf16[512,288]{1,0:T(8,128)(2,1)S(1)}, bf16[512,288]{1,0:T(8,128)(2,1)}, u32[]{:S(2)}) copy-start(bf16[512,288]{1,0:T(8,128)(2,1)} %get-tuple-element.16) | copy-start | bytes 884740
  138.7 0.9 copy-start.11
  138.7 0.8 copy-start.12
  145.3 1.0 copy-start.5
  146.3 1.0 copy-start.7
  152.3 0.9 copy-start.13
  153.2 91.7 %collective-permute-start.6 = (bf16[512,128]{1,0:T(8,128)(2,1)S(1)}, bf16[512,128]{1,0:T(8,128)(2,1)S(1)}, u32[]{:S(2)}, u32[]{:S(2)}) collective-permute-start(bf16[512,128]{1,0:T(8,128)(2,1)S(1)} %bitcast.50), channel_id=1, source_target_pairs={{0,4},{4,8},{8,12},{12,16},{16,20},{20,24},{24,28},{28,0},{1,5},{5... | collective-permute-start | bytes 393224 | tf_op jit(solution)/shard_map/ppermute | solution.py:32
  153.3 72.6 %collective-permute-start.4 = (bf16[512,128]{1,0:T(8,128)(2,1)S(1)}, bf16[512,128]{1,0:T(8,128)(2,1)S(1)}, u32[]{:S(2)}, u32[]{:S(2)}) collective-permute-start(bf16[512,128]{1,0:T(8,128)(2,1)S(1)} %bitcast.51), channel_id=1, source_target_pairs={{0,28},{4,0},{8,4},{12,8},{16,12},{20,16},{24,20},{28,24},{1,29},{... | collective-permute-start | bytes 393224 | tf_op jit(solution)/shard_map/ppermute | solution.py:32
  155.8 70.4 %collective-permute-start.7 = (bf16[512,128]{1,0:T(8,128)(2,1)S(1)}, bf16[512,128]{1,0:T(8,128)(2,1)S(1)}, u32[]{:S(2)}, u32[]{:S(2)}) collective-permute-start(bf16[512,128]{1,0:T(8,128)(2,1)S(1)} %bitcast.52), channel_id=1, source_target_pairs={{0,16},{4,20},{8,24},{12,28},{16,0},{20,4},{24,8},{28,12},{1,17},{... | collective-permute-start | bytes 393224 | tf_op jit(solution)/shard_map/ppermute | solution.py:32
  223.0 3.0 %copy-start.8 = (bf16[3,512,512]{2,1,0:T(8,128)(2,1)S(1)}, bf16[3,512,512]{2,1,0:T(8,128)(2,1)}, u32[]{:S(2)}) copy-start(bf16[3,512,512]{2,1,0:T(8,128)(2,1)} %all-reduce.2.cloned.1.call-done) | copy-start | bytes 4718596
  224.3 20.6 %collective-permute-start.5 = (bf16[512,512]{1,0:T(8,128)(2,1)S(1)}, bf16[512,512]{1,0:T(8,128)(2,1)S(1)}, u32[]{:S(2)}, u32[]{:S(2)}) collective-permute-start(bf16[512,512]{1,0:T(8,128)(2,1)S(1)} %get-tuple-element.17), channel_id=1, source_target_pairs={{0,4},{4,8},{8,12},{12,16},{16,20},{20,24},{24,28},{28,0},{1,5},{5... | collective-permute-start | bytes 1572872 | tf_op jit(solution)/shard_map/ppermute | solution.py:32
  224.4 20.1 %collective-permute-start.8 = (bf16[512,512]{1,0:T(8,128)(2,1)S(1)}, bf16[512,512]{1,0:T(8,128)(2,1)S(1)}, u32[]{:S(2)}, u32[]{:S(2)}) collective-permute-start(bf16[512,512]{1,0:T(8,128)(2,1)S(1)} %get-tuple-element.18), channel_id=1, source_target_pairs={{0,16},{4,20},{8,24},{12,28},{16,0},{20,4},{24,8},{28,12},{1,17},{... | collective-permute-start | bytes 1572872 | tf_op jit(solution)/shard_map/ppermute | solution.py:32
  245.3 2.6 collective-permute-start.9
  245.3 7.3 %collective-permute-start.11 = (bf16[512,128]{1,0:T(8,128)(2,1)S(1)}, bf16[512,128]{1,0:T(8,128)(2,1)S(1)}, u32[]{:S(2)}, u32[]{:S(2)}) collective-permute-start(bf16[512,128]{1,0:T(8,128)(2,1)S(1)} %fusion.15), channel_id=1, source_target_pairs={{0,16},{4,20},{8,24},{12,28},{16,0},{20,4},{24,8},{28,12},{1,17},{... | collective-permute-start | bytes 393224 | tf_op jit(solution)/shard_map/ppermute | solution.py:32
  246.9 6.4 %collective-permute-start.10 = (bf16[512,128]{1,0:T(8,128)(2,1)S(1)}, bf16[512,128]{1,0:T(8,128)(2,1)S(1)}, u32[]{:S(2)}, u32[]{:S(2)}) collective-permute-start(bf16[512,128]{1,0:T(8,128)(2,1)S(1)} %fusion.15), channel_id=1, source_target_pairs={{0,4},{4,8},{8,12},{12,16},{16,20},{20,24},{24,28},{28,0},{1,5},{5... | collective-permute-start | bytes 393224 | tf_op jit(solution)/shard_map/ppermute | solution.py:32
  253.7 5.0 %collective-permute-start.14 = (bf16[512,128]{1,0:T(8,128)(2,1)S(1)}, bf16[512,128]{1,0:T(8,128)(2,1)S(1)}, u32[]{:S(2)}, u32[]{:S(2)}) collective-permute-start(bf16[512,128]{1,0:T(8,128)(2,1)S(1)} %fusion.14), channel_id=1, source_target_pairs={{0,16},{4,20},{8,24},{12,28},{16,0},{20,4},{24,8},{28,12},{1,17},{... | collective-permute-start | bytes 393224 | tf_op jit(solution)/shard_map/ppermute | solution.py:32
  255.2 6.1 %collective-permute-start.13 = (bf16[512,128]{1,0:T(8,128)(2,1)S(1)}, bf16[512,128]{1,0:T(8,128)(2,1)S(1)}, u32[]{:S(2)}, u32[]{:S(2)}) collective-permute-start(bf16[512,128]{1,0:T(8,128)(2,1)S(1)} %fusion.14), channel_id=1, source_target_pairs={{0,4},{4,8},{8,12},{12,16},{16,20},{20,24},{24,28},{28,0},{1,5},{5... | collective-permute-start | bytes 393224 | tf_op jit(solution)/shard_map/ppermute | solution.py:32
  255.2 5.2 %collective-permute-start.12 = (bf16[512,128]{1,0:T(8,128)(2,1)S(1)}, bf16[512,128]{1,0:T(8,128)(2,1)S(1)}, u32[]{:S(2)}, u32[]{:S(2)}) collective-permute-start(bf16[512,128]{1,0:T(8,128)(2,1)S(1)} %fusion.14), channel_id=1, source_target_pairs={{0,28},{4,0},{8,4},{12,8},{16,12},{20,16},{24,20},{28,24},{1,29},{... | collective-permute-start | bytes 393224 | tf_op jit(solution)/shard_map/ppermute | solution.py:32
Sparse Core Ops, SparseCore 0:
  152.4 70.4 all-reduce.1

commit v3 on v2

--- a/solution.py
+++ b/solution.py
@@ -284,8 +284,140 @@
     return (apply_blocks(terms, current) - SHIFT_CENTER * current.astype(jnp.float32)) / HALF_WIDTH
 
 
+def reduce_kernel(
+    slabs, elements, part_ref, out_ref, mirror_ref, slots, sum_s, sum_r, gather_s, gather_r, mirror_s, mirror_r
+):
+    me, element = lax.axis_index("band"), lax.axis_index("elem")
+    share = part_ref.shape[1] // slabs
+    half = share // 2
+
+    def along(axis, place, by, count):
+        return {axis: lax.rem(place + by + count, count)}
+
+    def rows(steps, ring):
+        chunk = lax.rem(me + steps + 2 * slabs, slabs)
+        return pl.ds(pl.multiple_of(chunk * share + ring * half, half), half)
+
+    def copy(source, target, send, receive, device):
+        return pltpu.make_async_remote_copy(
+            src_ref=source,
+            dst_ref=target,
+            send_sem=send,
+            recv_sem=receive,
+            device_id=device,
+            device_id_type=pl.DeviceIdType.MESH,
+        )
+
+    barrier = pltpu.get_barrier_semaphore()
+    for axis, place, by, count in (
+        ("band", me, 1, slabs),
+        ("band", me, -1, slabs),
+        ("elem", element, -1, elements),
+        ("elem", element, -EB, elements),
+    ):
+        pl.semaphore_signal(
+            barrier,
+            inc=1,
+            device_id=along(axis, place, by, count),
+            device_id_type=pl.DeviceIdType.MESH,
+        )
+    pl.semaphore_wait(barrier, 4)
+
+    sent = []
+    ways = (1, -1)
+    for step in range(slabs - 1):
+        moving = []
+        for ring, way in enumerate(ways):
+            source = slots.at[ring, step - 1] if step else part_ref.at[:, rows(-way, ring), :]
+            moving.append(
+                copy(
+                    source,
+                    slots.at[ring, step],
+                    sum_s.at[ring, step],
+                    sum_r.at[ring, step],
+                    along("band", me, way, slabs),
+                )
+            )
+            moving[-1].start()
+        for ring, way in enumerate(ways):
+            moving[ring].wait_recv()
+            place = rows(-way * (step + 2), ring)
+            total = slots[ring, step].astype(jnp.float32) + part_ref[:, place, :].astype(jnp.float32)
+            if step < slabs - 2:
+                slots[ring, step] = total.astype(jnp.bfloat16)
+            else:
+                out_ref[:, place, :] = total.astype(jnp.bfloat16)
+        sent += moving
+
+    mirrors = []
+
+    def hand_on(step, ring, way):
+        place = rows(-way * step, ring)
+        for which, by in enumerate((1, EB)):
+            mirrors.append(
+                copy(
+                    out_ref.at[which + 1, place, :],
+                    mirror_ref.at[which, place, :],
+                    mirror_s.at[ring, step, which],
+                    mirror_r.at[ring, step, which],
+                    along("elem", element, by, elements),
+                )
+            )
+            mirrors[-1].start()
+
+    for step in range(slabs - 1):
+        moving = []
+        for ring, way in enumerate(ways):
+            place = rows(-way * step, ring)
+            moving.append(
+                copy(
+                    out_ref.at[:, place, :],
+                    out_ref.at[:, place, :],
+                    gather_s.at[ring, step],
+                    gather_r.at[ring, step],
+                    along("band", me, way, slabs),
+                )
+            )
+            moving[-1].start()
+        for ring, way in enumerate(ways):
+            hand_on(step, ring, way)
+        for ring in range(2):
+            moving[ring].wait_recv()
+        sent += moving
+    for ring, way in enumerate(ways):
+        hand_on(slabs - 1, ring, way)
+    for one in sent:
+        one.wait_send()
+    for one in mirrors:
+        one.wait()
+
+
 def summed_blocks(partials):
-    return lax.psum(partials, "band")
+    slabs, elements = lax.axis_size("band"), lax.axis_size("elem")
+    kinds, count, width = partials.shape
+    half = count // slabs // 2
+    whole = pl.BlockSpec(memory_space=pltpu.VMEM)
+    return pl.pallas_call(
+        functools.partial(reduce_kernel, slabs, elements),
+        in_specs=[whole],
+        out_specs=[whole, whole],
+        out_shape=[
+            jax.ShapeDtypeStruct(partials.shape, jnp.bfloat16),
+            jax.ShapeDtypeStruct((kinds - 1, count, width), jnp.bfloat16),
+        ],
+        scratch_shapes=[
+            pltpu.VMEM((2, slabs - 1, kinds, half, width), jnp.bfloat16),
+            pltpu.SemaphoreType.DMA((2, slabs - 1)),
+            pltpu.SemaphoreType.DMA((2, slabs - 1)),
+            pltpu.SemaphoreType.DMA((2, slabs - 1)),
+            pltpu.SemaphoreType.DMA((2, slabs - 1)),
+            pltpu.SemaphoreType.DMA((2, slabs, kinds - 1)),
+            pltpu.SemaphoreType.DMA((2, slabs, kinds - 1)),
+        ],
+        compiler_params=pltpu.CompilerParams(
+            collective_id=0, has_side_effects=True, vmem_limit_bytes=VMEM_LIMIT
+        ),
+    )(partials)
 
 
 def on_device(orbitals, potential, basis_count, states):
@@ -314,10 +446,7 @@
     near = jnp.concatenate([last[:, :half], after, initial[:, half:], before], axis=1)
     far = jnp.concatenate([after, last[:, :half], before, initial[:, half:]], axis=1)
     partials = partial_blocks(inner, near, far, lz, rz, ly, ry)
-    summed = summed_blocks(partials)
-    mirrored = []
-    for position, offset in ((1, 1), (2, EB)):
-        mirrored.append(from_behind(summed[position], "elem", offset))
+    summed, mirrored = summed_blocks(partials)
     terms = [(summed[0], 1), (summed[1], 1), (mirrored[0], 0), (summed[2], 1), (mirrored[1], 0)]
     start_states = states[0]
     first_term = scaled(terms, start_states).astype(jnp.bfloat16)

time: 270 us -> 239 us (0.89)
  waiting for transfers between devices: 170 us -> 83.9 us
  Pallas kernels: 37.7 us -> 104 us
  between operations: 14.3 us -> 0.91 us
  matrix products: 4.73 us -> 8.33 us
    pallas_call x0 -> x1, Pallas kernels: none -> 66 us  [summed_blocks(): pl.pallas_call(functools.partial(reduce_kernel, slabs, elements), in_spec...]
    psum x1 -> x0, waiting for transfers between devices: 65.6 us -> none  [summed_blocks(): return lax.psum(partials, 'band')]
    ppermute x13 -> x11, waiting for transfers between devices: 24.9 us -> 4.78 us  [from_behind(): lax.ppermute(value, axis, [(i, (i + by) % devices) for i in range(devices)])]
    dot_general x15, matrix products: 4.73 us -> 8.33 us  [apply_blocks(): lax.dot_general(matrix, source, (((contract,), (0,)), ((), ())), preferre...]
    ppermute x13 -> x11, starting transfers between devices: 13.4 us -> 12.6 us  [from_behind(): lax.ppermute(value, axis, [(i, (i + by) % devices) for i in range(devices)])]
    unnamed x28 -> x26, local copies, waits for them, and re-layouts: 9.76 us -> 9.45 us
  transfers between devices with their start and end apart: 17 -> 14, of which waited for: 7 -> 4; matrix products, arithmetic and copies ran while one was open for 4% -> 6% of each run, Pallas kernels for 4% -> 36%
where the time goes in v3:
time: 239 us; the launch traced here: 238 us
  Pallas kernels  104 us (44%)
  waiting for transfers between devices  83.9 us (35%)
  starting transfers between devices  22.2 us (9%)
  local copies, waits for them, and re-layouts  16.9 us (7%)
  matrix products  8.33 us (3%)
  other arithmetic  2.39 us (1%)
    all_to_all x1, waiting for transfers between devices, on_device(): lax.all_to_all(basis, 'band', split_axis=0, concat_axis=0, tiled=True)  79.1 us
    pallas_call x1, Pallas kernels, summed_blocks(): pl.pallas_call(functools.partial(reduce_kernel, slabs, elements), in_spec...  66 us
    pallas_call x1, Pallas kernels, filtered_basis(): pl.pallas_call(functools.partial(filter_kernel, slabs), in_specs=[pl.Bloc...  17.7 us
    ppermute x11, starting transfers between devices, from_behind(): lax.ppermute(value, axis, [(i, (i + by) % devices) for i in range(devices)])  12.6 us
    pallas_call x1, Pallas kernels, interior_block(): pl.pallas_call(interior_kernel, grid=(2,), in_specs=[pl.BlockSpec((count,...  9.77 us
    unnamed x26, local copies, waits for them, and re-layouts  9.45 us
    dot_general x15, matrix products, apply_blocks(): lax.dot_general(matrix, source, (((contract,), (0,)), ((), ())), preferre...  8.33 us
    all_to_all x1, starting transfers between devices, on_device(): lax.all_to_all(basis, 'band', split_axis=0, concat_axis=0, tiled=True)  6.32 us
  transfers between devices with their start and end apart: 14, of which 4 were waited for; matrix products, arithmetic and copies ran while one was open for 6% of the time, Pallas kernels for 36%

profile of v3, /device:TPU:0, one launch (start us, length us, event | category | flops | bytes accessed | tf_op | source)
XLA Modules:
  0.0 238.2 jit_solution(16496173538000835367)
XLA Ops:
  0.7 0.9 add_multiply_fusion.diag_ref
  1.6 17.7 %shard_map.64 = bf16[4,128,3456]{2,1,0:T(8,128)(2,1)S(1)} custom-call(s32[2]{0:T(128)S(1)} %pad_add_fusion.bounds_ref, bf16[128,13824]{1,0:T(8,128)(2,1)} %bitcast.65, f32[1,13824]{1,0:T(1,128)S(1)} %add_multiply_fusion.diag_ref, bf16[9,1280,256]{2,1,0:T(8,128)(2,1)} %constant.42.clone.table_ref), custom_call_target="tpu_custom_call" | custom-call | tf_op jit(solution)/shard_map/pallas_call | solution.py:129
  19.3 1.7 copy-done.2
  21.1 6.3 %all-to-all-start = ((bf16[4,128,3456]{2,1,0:T(8,128)(2,1)}), bf16[4,128,3456]{2,1,0:T(8,128)(2,1)S(1)}, u32[]{:S(2)}, u32[]{:S(2)}) async-start(bf16[4,128,3456]{2,1,0:T(8,128)(2,1)} %copy-done.2), calls=%async_computation | async-start | bytes 7077888 | tf_op jit(solution)/shard_map/all_to_all | solution.py:430
  27.4 79.1 %all-to-all-done = bf16[4,128,3456]{2,1,0:T(8,128)(2,1)S(1)} async-done(((bf16[4,128,3456]{2,1,0:T(8,128)(2,1)}), bf16[4,128,3456]{2,1,0:T(8,128)(2,1)S(1)}, u32[]{:S(2)}, u32[]{:S(2)}) %all-to-all-start) | async-done | bytes 3538976 | tf_op jit(solution)/shard_map/all_to_all | solution.py:430
  106.5 1.3 fusion.57
  107.8 0.7 copy-done
  108.6 5.2 %shard_map.66 = (bf16[512,384]{1,0:T(8,128)(2,1)S(1)}, bf16[512,384]{1,0:T(8,128)(2,1)}, bf16[512,384]{1,0:T(8,128)(2,1)S(1)}, bf16[512,384]{1,0:T(8,128)(2,1)}) custom-call(bf16[512,3456]{1,0:T(8,128)(2,1)} %bitcast.62, bf16[1152,512]{1,0:T(8,128)(2,1)S(1)} %copy-done.4), custom_call_target="tpu_custom_call" | custom-call | tf_op jit(solution)/shard_map/pallas_call | solution.py:184
  113.8 0.8 copy-done.5
  114.6 0.8 copy-done.7
  115.4 2.0 collective-permute-start.1
  117.4 1.3 collective-permute-start
  118.7 1.2 collective-permute-start.2
  119.8 0.5 collective-permute-start.3
  120.4 0.7 dynamic-slice_add_fusion.diag_ref
  121.1 2.0 copy-done.1
  123.1 9.8 %shard_map.65.inner_ref = f32[512,512]{1,0:T(8,128)S(1)} custom-call(bf16[512,3456]{1,0:T(8,128)(2,1)S(1)} %bitcast.63, bf16[512,3456]{1,0:T(8,128)(2,1)S(1)} %bitcast.64, f32[1,3456]{1,0:T(1,128)S(1)} %dynamic-slice_add_fusion.diag_ref, bf16[9,1280,256]{2,1,0:T(8,128)(2,1)} %constant.42.clone.table_ref), custom_call_target="tpu_custom_call" | custom-call | tf_op jit(solution)/shard_map/pallas_call | solution.py:218
  132.9 1.2 collective-permute-start.4
  134.1 1.5 collective-permute-start.6
  135.7 3.1 %concatenate.7.far_ref = bf16[512,1152]{1,0:T(8,128)(2,1)S(1)} concatenate(bf16[512,288]{1,0:T(8,128)(2,1)S(1)} %collective-permute-done, bf16[512,288]{1,0:T(8,128)(2,1)S(1)} %copy-done.10, bf16[512,288]{1,0:T(8,128)(2,1)} %collective-permute-done.1, bf16[512,288]{1,0:T(8,128)(2,1)S(1)} %copy-done.9), dimensions={1} | concatenate | bytes 2359296 | tf_op jit(solution)/shard_map/concatenate | solution.py:447
  138.8 2.9 %concatenate.6.near_ref = bf16[512,1152]{1,0:T(8,128)(2,1)S(1)} concatenate(bf16[512,288]{1,0:T(8,128)(2,1)} %get-tuple-element.20, bf16[512,288]{1,0:T(8,128)(2,1)} %copy-done.11, bf16[512,288]{1,0:T(8,128)(2,1)} %get-tuple-element.18, bf16[512,288]{1,0:T(8,128)(2,1)} %collective-permute-done.1), dimensions={1} | concatenate | bytes 2359296 | tf_op jit(solution)/shard_map/concatenate | solution.py:446
  141.8 1.0 copy-done.6
  142.8 1.0 copy-done.8
  143.8 5.0 %shard_map.67.part_ref = bf16[3,512,512]{2,1,0:T(8,128)(2,1)} custom-call(f32[512,512]{1,0:T(8,128)S(1)} %shard_map.65.inner_ref, bf16[512,1152]{1,0:T(8,128)(2,1)S(1)} %concatenate.6.near_ref, bf16[512,1152]{1,0:T(8,128)(2,1)S(1)} %concatenate.7.far_ref, bf16[512,384]{1,0:T(8,128)(2,1)S(1)} %copy-done.6, bf16[512,384]{1,0:T(8,128)(2,1)} %collective-permute-done.2.rz_ref, ...), custom_call_target="tpu_custom_call" | custom-call | tf_op jit(solution)/shard_map/pallas_call | solution.py:258
  148.7 1.4 copy-done.3
  150.1 66.0 %shard_map.68 = (bf16[3,512,512]{2,1,0:T(8,128)(2,1)S(1)}, bf16[2,512,512]{2,1,0:T(8,128)(2,1)S(1)}) custom-call(bf16[3,512,512]{2,1,0:T(8,128)(2,1)S(1)} %copy-done.3), custom_call_target="tpu_custom_call" | custom-call | tf_op jit(solution)/shard_map/pallas_call | solution.py:400
  216.1 0.3 fusion.38
  216.4 1.2 fusion.26
  217.6 1.2 convolution_add_fusion.5
  218.8 1.2 fusion.20
  220.1 1.3 fusion.15
  221.3 1.3 collective-permute-start.9
  222.6 2.6 %collective-permute-start.7 = (bf16[512,128]{1,0:T(8,128)(2,1)S(1)}, bf16[512,128]{1,0:T(8,128)(2,1)S(1)}, u32[]{:S(2)}, u32[]{:S(2)}) collective-permute-start(bf16[512,128]{1,0:T(8,128)(2,1)S(1)} %fusion.15), channel_id=1, source_target_pairs={{0,28},{4,0},{8,4},{12,8},{16,12},{20,16},{24,20},{28,24},{1,29},{... | collective-permute-start | bytes 393224 | tf_op jit(solution)/shard_map/ppermute | solution.py:32
  225.5 0.8 collective-permute-done.9
  226.4 0.3 fusion.18
  226.7 1.1 collective-permute-done.7
  228.1 0.3 fusion.24
  228.4 0.4 fusion.14
  228.7 1.6 collective-permute-start.12
  230.4 0.3 collective-permute-start.11
  230.7 2.3 collective-permute-start.10
  233.0 0.3 fusion.34
  233.3 2.9 %collective-permute-done.12 = bf16[512,128]{1,0:T(8,128)(2,1)S(1)} collective-permute-done((bf16[512,128]{1,0:T(8,128)(2,1)S(1)}, bf16[512,128]{1,0:T(8,128)(2,1)S(1)}, u32[]{:S(2)}, u32[]{:S(2)}) %collective-permute-start.12) | collective-permute-done | bytes 131104 | tf_op jit(solution)/shard_map/ppermute | solution.py:32
  236.2 0.3 fusion.16
  236.5 0.3 convolution_add_fusion.1
  236.8 0.3 fusion.22
  237.1 0.4 multiply_reduce_fusion
  237.5 0.7 fusion.55
  (34 shorter events, 0.9 us)
Async XLA Ops:
  19.3 1.7 copy-start.2
  21.1 85.4 %all-to-all-start = ((bf16[4,128,3456]{2,1,0:T(8,128)(2,1)}), bf16[4,128,3456]{2,1,0:T(8,128)(2,1)S(1)}, u32[]{:S(2)}, u32[]{:S(2)}) async-start(bf16[4,128,3456]{2,1,0:T(8,128)(2,1)} %copy-done.2), calls=%async_computation | async-start | bytes 7077888 | tf_op jit(solution)/shard_map/all_to_all | solution.py:430
  27.4 192.7 %collective-permute-start.5 = (bf16[512,128]{1,0:T(8,128)(2,1)}, bf16[512,128]{1,0:T(8,128)(2,1)}, u32[]{:S(2)}, u32[]{:S(2)}) collective-permute-start(bf16[512,128]{1,0:T(8,128)(2,1)} %bitcast.66), channel_id=1, source_target_pairs={{0,4},{4,8},{8,12},{12,16},{16,20},{20,24},{24,28},{28,0},{1,5},{5... | collective-permute-start | bytes 393224 | tf_op jit(solution)/shard_map/ppermute | solution.py:32
  106.5 2.0 copy-start
  106.5 2.1 copy-start.4
  113.8 0.8 copy-start.5
  114.6 0.8 copy-start.7
  115.4 17.5 %collective-permute-start.1 = (bf16[512,288]{1,0:T(8,128)(2,1)S(1)}, bf16[512,288]{1,0:T(8,128)(2,1)}, u32[]{:S(2)}, u32[]{:S(2)}) collective-permute-start(bf16[512,288]{1,0:T(8,128)(2,1)S(1)} %get-tuple-element.17), channel_id=1, source_target_pairs={{0,1},{1,2},{2,3},{4,5},{5,6},{6,7},{8,9},{9,10},{10,11},{12,13},{... | collective-permute-start | bytes 884744 | tf_op jit(solution)/shard_map/ppermute | solution.py:441
  117.4 16.7 %collective-permute-start = (bf16[512,288]{1,0:T(8,128)(2,1)S(1)}, bf16[512,288]{1,0:T(8,128)(2,1)S(1)}, u32[]{:S(2)}, u32[]{:S(2)}) collective-permute-start(bf16[512,288]{1,0:T(8,128)(2,1)S(1)} %get-tuple-element.19), channel_id=1, source_target_pairs={{1,0},{2,1},{3,2},{5,4},{6,5},{7,6},{9,8},{10,9},{11,10},{13,12},{... | collective-permute-start | bytes 884744 | tf_op jit(solution)/shard_map/ppermute | solution.py:440
  118.7 23.1 %collective-permute-start.2 = (bf16[512,384]{1,0:T(8,128)(2,1)}, bf16[512,384]{1,0:T(8,128)(2,1)}, u32[]{:S(2)}, u32[]{:S(2)}) collective-permute-start(bf16[512,384]{1,0:T(8,128)(2,1)} %get-tuple-element.12), channel_id=1, source_target_pairs={{0,28},{4,0},{8,4},{12,8},{16,12},{20,16},{24,20},{28,24},{1,29},{... | collective-permute-start | bytes 1179656 | tf_op jit(solution)/shard_map/ppermute | solution.py:32
  119.8 21.9 %collective-permute-start.3 = (bf16[512,384]{1,0:T(8,128)(2,1)}, bf16[512,384]{1,0:T(8,128)(2,1)}, u32[]{:S(2)}, u32[]{:S(2)}) collective-permute-start(bf16[512,384]{1,0:T(8,128)(2,1)} %get-tuple-element.14), channel_id=1, source_target_pairs={{0,16},{4,20},{8,24},{12,28},{16,0},{20,4},{24,8},{28,12},{1,17},{... | collective-permute-start | bytes 1179656 | tf_op jit(solution)/shard_map/ppermute | solution.py:32
  121.1 2.0 copy-start.1
  123.1 9.8 %copy-start.12 = (bf16[1,512,128]{2,1,0:T(8,128)(2,1)S(1)}, bf16[1,512,128]{2,1,0:T(8,128)(2,1)}, u32[]{:S(2)}) copy-start(bf16[1,512,128]{2,1,0:T(8,128)(2,1)} %param.9) | copy-start | bytes 393220
  123.1 12.6 %copy-start.9 = (bf16[512,288]{1,0:T(8,128)(2,1)S(1)}, bf16[512,288]{1,0:T(8,128)(2,1)}, u32[]{:S(2)}) copy-start(bf16[512,288]{1,0:T(8,128)(2,1)} %get-tuple-element.18) | copy-start | bytes 884740
  123.1 12.6 %copy-start.10 = (bf16[512,288]{1,0:T(8,128)(2,1)S(1)}, bf16[512,288]{1,0:T(8,128)(2,1)}, u32[]{:S(2)}) copy-start(bf16[512,288]{1,0:T(8,128)(2,1)} %get-tuple-element.20) | copy-start | bytes 884740
  132.9 84.7 %collective-permute-start.4 = (bf16[512,128]{1,0:T(8,128)(2,1)S(1)}, bf16[512,128]{1,0:T(8,128)(2,1)}, u32[]{:S(2)}, u32[]{:S(2)}) collective-permute-start(bf16[512,128]{1,0:T(8,128)(2,1)S(1)} %bitcast.67), channel_id=1, source_target_pairs={{0,28},{4,0},{8,4},{12,8},{16,12},{20,16},{24,20},{28,24},{1,29},{... | collective-permute-start | bytes 393224 | tf_op jit(solution)/shard_map/ppermute | solution.py:32
  134.1 1.5 copy-start.11
  134.1 82.3 %collective-permute-start.6 = (bf16[512,128]{1,0:T(8,128)(2,1)S(1)}, bf16[512,128]{1,0:T(8,128)(2,1)}, u32[]{:S(2)}, u32[]{:S(2)}) collective-permute-start(bf16[512,128]{1,0:T(8,128)(2,1)S(1)} %bitcast.68), channel_id=1, source_target_pairs={{0,16},{4,20},{8,24},{12,28},{16,0},{20,4},{24,8},{28,12},{1,17},{... | collective-permute-start | bytes 393224 | tf_op jit(solution)/shard_map/ppermute | solution.py:32
  141.8 1.0 copy-start.6
  142.8 1.0 copy-start.8
  148.7 1.4 copy-start.3
  221.3 5.0 %collective-permute-start.9 = (bf16[512,128]{1,0:T(8,128)(2,1)S(1)}, bf16[512,128]{1,0:T(8,128)(2,1)S(1)}, u32[]{:S(2)}, u32[]{:S(2)}) collective-permute-start(bf16[512,128]{1,0:T(8,128)(2,1)S(1)} %fusion.15), channel_id=1, source_target_pairs={{0,16},{4,20},{8,24},{12,28},{16,0},{20,4},{24,8},{28,12},{1,17},{... | collective-permute-start | bytes 393224 | tf_op jit(solution)/shard_map/ppermute | solution.py:32
  222.6 5.8 %collective-permute-start.8 = (bf16[512,128]{1,0:T(8,128)(2,1)S(1)}, bf16[512,128]{1,0:T(8,128)(2,1)S(1)}, u32[]{:S(2)}, u32[]{:S(2)}) collective-permute-start(bf16[512,128]{1,0:T(8,128)(2,1)S(1)} %fusion.15), channel_id=1, source_target_pairs={{0,4},{4,8},{8,12},{12,16},{16,20},{20,24},{24,28},{28,0},{1,5},{5... | collective-permute-start | bytes 393224 | tf_op jit(solution)/shard_map/ppermute | solution.py:32
  222.6 5.2 %collective-permute-start.7 = (bf16[512,128]{1,0:T(8,128)(2,1)S(1)}, bf16[512,128]{1,0:T(8,128)(2,1)S(1)}, u32[]{:S(2)}, u32[]{:S(2)}) collective-permute-start(bf16[512,128]{1,0:T(8,128)(2,1)S(1)} %fusion.15), channel_id=1, source_target_pairs={{0,28},{4,0},{8,4},{12,8},{16,12},{20,16},{24,20},{28,24},{1,29},{... | collective-permute-start | bytes 393224 | tf_op jit(solution)/shard_map/ppermute | solution.py:32
  228.7 7.4 %collective-permute-start.12 = (bf16[512,128]{1,0:T(8,128)(2,1)S(1)}, bf16[512,128]{1,0:T(8,128)(2,1)S(1)}, u32[]{:S(2)}, u32[]{:S(2)}) collective-permute-start(bf16[512,128]{1,0:T(8,128)(2,1)S(1)} %fusion.14), channel_id=1, source_target_pairs={{0,16},{4,20},{8,24},{12,28},{16,0},{20,4},{24,8},{28,12},{1,17},{... | collective-permute-start | bytes 393224 | tf_op jit(solution)/shard_map/ppermute | solution.py:32
  230.4 6.8 %collective-permute-start.11 = (bf16[512,128]{1,0:T(8,128)(2,1)S(1)}, bf16[512,128]{1,0:T(8,128)(2,1)S(1)}, u32[]{:S(2)}, u32[]{:S(2)}) collective-permute-start(bf16[512,128]{1,0:T(8,128)(2,1)S(1)} %fusion.14), channel_id=1, source_target_pairs={{0,4},{4,8},{8,12},{12,16},{16,20},{20,24},{24,28},{28,0},{1,5},{5... | collective-permute-start | bytes 393224 | tf_op jit(solution)/shard_map/ppermute | solution.py:32
  230.7 5.9 %collective-permute-start.10 = (bf16[512,128]{1,0:T(8,128)(2,1)S(1)}, bf16[512,128]{1,0:T(8,128)(2,1)S(1)}, u32[]{:S(2)}, u32[]{:S(2)}) collective-permute-start(bf16[512,128]{1,0:T(8,128)(2,1)S(1)} %fusion.14), channel_id=1, source_target_pairs={{0,28},{4,0},{8,4},{12,8},{16,12},{20,16},{24,20},{28,24},{1,29},{... | collective-permute-start | bytes 393224 | tf_op jit(solution)/shard_map/ppermute | solution.py:32

commit v4 on v3

--- a/solution.py
+++ b/solution.py
@@ -162,134 +162,39 @@
     return jnp.asarray(np.concatenate(parts, axis=1).astype(ml_dtypes.bfloat16))
 
 
-def faces_kernel(rows_ref, select_ref, lz_ref, rz_ref, ly_ref, ry_ref):
-    chunk = select_ref.shape[0]
-    group = select_ref.shape[1] // 4
-    for which in range(rows_ref.shape[1] // chunk):
-        picked = jnp.dot(
-            rows_ref[:, which * chunk : (which + 1) * chunk],
-            select_ref[...],
-            preferred_element_type=jnp.float32,
-        ).astype(jnp.bfloat16)
-        for place, out in enumerate((lz_ref, rz_ref, ly_ref, ry_ref)):
-            out[:, which * group : (which + 1) * group] = picked[:, place * group : (place + 1) * group]
-
-
-def face_layers(rows):
-    count, length = rows.shape
-    chunk = face_chunk(length)
-    select = face_selector(chunk)
-    width = length // chunk * (select.shape[1] // 4)
-    step = count // 4
-    return pl.pallas_call(
-        faces_kernel,
-        grid=(4,),
-        in_specs=[
-            pl.BlockSpec((step, length), lambda i: (i, 0)),
-            pl.BlockSpec(select.shape, lambda i: (0, 0)),
-        ],
-        out_specs=[pl.BlockSpec((step, width), lambda i: (i, 0))] * 4,
-        out_shape=[jax.ShapeDtypeStruct((count, width), jnp.bfloat16)] * 4,
-        compiler_params=pltpu.CompilerParams(vmem_limit_bytes=VMEM_LIMIT),
-    )(rows, select)
-
-
-def interior_kernel(all_ref, rows_ref, diag_ref, table_ref, out_ref, wide_ref, applied_ref):
-    count, length = rows_ref.shape
-    clear_pads(wide_ref, length)
-    wide_ref[:, PAD : PAD + length] = rows_ref[...]
-    for at in range(0, length, TILE):
-        size = min(TILE, length - at)
-        total = jnp.dot(
-            windows(wide_ref, at), table_ref[at // TILE % PERIOD], preferred_element_type=jnp.float32
-        )
-        applied_ref[:, at : at + size] = (
-            diag_ref[0:1, at : at + size] * rows_ref[:, at : at + size].astype(jnp.float32)
-            - total[:, :size]
-        ).astype(jnp.bfloat16)
-    out_ref[...] = lax.dot_general(
-        applied_ref[...], all_ref[...], NT, preferred_element_type=jnp.float32
-    )
-
-
-def interior_block(rows, slab_potential, table):
-    count, length = rows.shape
-    step = count // 2
-    return pl.pallas_call(
-        interior_kernel,
-        grid=(2,),
-        in_specs=[
-            pl.BlockSpec((count, length), lambda i: (0, 0)),
-            pl.BlockSpec((step, length), lambda i: (i, 0)),
-            pl.BlockSpec((1, length), lambda i: (0, 0)),
-            pl.BlockSpec(table.shape, lambda i: (0, 0, 0)),
-        ],
-        out_specs=pl.BlockSpec((step, count), lambda i: (i, 0)),
-        out_shape=jax.ShapeDtypeStruct((count, count), jnp.float32),
-        scratch_shapes=[
-            pltpu.VMEM((step, padded_width(length)), jnp.bfloat16),
-            pltpu.VMEM((step, length), jnp.bfloat16),
-        ],
-        compiler_params=pltpu.CompilerParams(vmem_limit_bytes=VMEM_LIMIT),
-    )(rows, rows, (6.0 + slab_potential)[None], table)
-
-
-def partials_kernel(inner_ref, near_ref, far_ref, lz_ref, rz_ref, ly_ref, ry_ref, out_ref):
-    def product(a, b):
-        return lax.dot_general(a, b, NT, preferred_element_type=jnp.float32)
-
-    seam = product(near_ref[...], far_ref[...])
-    out_ref[0] = ((inner_ref[...] - seam) * (1.0 / G)).astype(jnp.bfloat16)
-    weight = -0.5 / PLANE
-    out_ref[1] = (product(lz_ref[...], rz_ref[...]) * weight).astype(jnp.bfloat16)
-    out_ref[2] = (product(ly_ref[...], ry_ref[...]) * weight).astype(jnp.bfloat16)
-
-
-def partial_blocks(inner, near, far, lz, rz, ly, ry):
-    count = inner.shape[0]
-    step = count // 4
-
-    def cut(value):
-        return pl.BlockSpec((step, value.shape[1]), lambda i: (i, 0))
-
-    def full(value):
-        return pl.BlockSpec(value.shape, lambda i: (0, 0))
-
-    return pl.pallas_call(
-        partials_kernel,
-        grid=(4,),
-        in_specs=[cut(inner), cut(near), full(far), cut(lz), full(rz), cut(ly), full(ry)],
-        out_specs=pl.BlockSpec((3, step, count), lambda i: (0, i, 0)),
-        out_shape=jax.ShapeDtypeStruct((3, count, count), jnp.bfloat16),
-        compiler_params=pltpu.CompilerParams(vmem_limit_bytes=VMEM_LIMIT),
-    )(inner, near, far, lz, rz, ly, ry)
-
-
-def apply_blocks(terms, current):
-    offsets = [0, 1, -1, EB, -EB]
-    running = jnp.zeros((terms[0][0].shape[0], current.shape[1]), jnp.float32)
-    for position, offset in enumerate(offsets):
-        matrix, contract = terms[position]
-        if offset == 0:
-            source = current
-        else:
-            source = from_behind(current, "elem", -offset)
-        running = running + lax.dot_general(
-            matrix, source, (((contract,), (0,)), ((), ())), preferred_element_type=jnp.float32
-        )
-    return running
-
-
-def scaled(terms, current):
-    return (apply_blocks(terms, current) - SHIFT_CENTER * current.astype(jnp.float32)) / HALF_WIDTH
-
-
-def reduce_kernel(
-    slabs, elements, part_ref, out_ref, mirror_ref, slots, sum_s, sum_r, gather_s, gather_r, mirror_s, mirror_r
+def blocks_kernel(
+    slabs,
+    elements,
+    rows_ref,
+    diag_ref,
+    table_ref,
+    select_ref,
+    out_ref,
+    mirror_ref,
+    wide_ref,
+    applied_ref,
+    inner_ref,
+    part_ref,
+    seam_refs,
+    face_refs,
+    slots,
+    seam_s,
+    seam_r,
+    face_s,
+    face_r,
+    sum_s,
+    sum_r,
+    gather_s,
+    gather_r,
+    mirror_s,
+    mirror_r,
 ):
     me, element = lax.axis_index("band"), lax.axis_index("elem")
     share = part_ref.shape[1] // slabs
     half = share // 2
+    functions, length = rows_ref.shape
+    last_ref, first_ref, up_ref, down_ref, after_ref, before_ref = seam_refs
+    lz_ref, rz_ref, ly_ref, ry_ref, rz_in, ry_in = face_refs
 
     def along(axis, place, by, count):
         return {axis: lax.rem(place + by + count, count)}
@@ -314,6 +219,8 @@
         ("band", me, -1, slabs),
         ("elem", element, -1, elements),
         ("elem", element, -EB, elements),
+        ("elem", element, 1, elements),
+        ("elem", element, EB, elements),
     ):
         pl.semaphore_signal(
             barrier,
@@ -321,7 +228,103 @@
             device_id=along(axis, place, by, count),
             device_id_type=pl.DeviceIdType.MESH,
         )
-    pl.semaphore_wait(barrier, 4)
+    pl.semaphore_wait(barrier, 6)
+
+    seam = PLANE // 2
+    down_ref[...] = rows_ref[:, 0:seam]
+    first_ref[...] = rows_ref[:, seam:PLANE]
+    last_ref[...] = rows_ref[:, length - PLANE : length - seam]
+    up_ref[...] = rows_ref[:, length - seam : length]
+    downward = copy(
+        down_ref, after_ref, seam_s.at[0], seam_r.at[0], along("band", me, -1, slabs)
+    )
+    upward = copy(up_ref, before_ref, seam_s.at[1], seam_r.at[1], along("band", me, 1, slabs))
+
+    @pl.when(me > 0)
+    def _():
+        downward.start()
+
+    @pl.when(me < slabs - 1)
+    def _():
+        upward.start()
+
+    chunk = select_ref.shape[0]
+    group = select_ref.shape[1] // 4
+    block = functions // 2
+
+    @pl.loop(0, 2)
+    def _(index):
+        here = pl.ds(pl.multiple_of(index * block, block), block)
+        for which in range(length // chunk):
+            picked = jnp.dot(
+                rows_ref[here, which * chunk : (which + 1) * chunk],
+                select_ref[...],
+                preferred_element_type=jnp.float32,
+            ).astype(jnp.bfloat16)
+            for place, face in enumerate((lz_ref, rz_ref, ly_ref, ry_ref)):
+                face[here, which * group : (which + 1) * group] = picked[
+                    :, place * group : (place + 1) * group
+                ]
+
+    faces = [
+        copy(rz_ref, rz_in, face_s.at[0], face_r.at[0], along("elem", element, -1, elements)),
+        copy(ry_ref, ry_in, face_s.at[1], face_r.at[1], along("elem", element, -EB, elements)),
+    ]
+    for one in faces:
+        one.start()
+
+    clear_pads(wide_ref, length)
+    wide_ref[:, PAD : PAD + length] = rows_ref[...]
+
+    @pl.loop(0, 2)
+    def _(index):
+        here = pl.ds(pl.multiple_of(index * block, block), block)
+        view = wide_ref.at[here]
+        for at in range(0, length, TILE):
+            size = min(TILE, length - at)
+            total = jnp.dot(
+                windows(view, at), table_ref[at // TILE % PERIOD], preferred_element_type=jnp.float32
+            )
+            applied_ref[:, at : at + size] = (
+                diag_ref[0:1, at : at + size] * rows_ref[here, at : at + size].astype(jnp.float32)
+                - total[:, :size]
+            ).astype(jnp.bfloat16)
+        inner_ref[here, :] = lax.dot_general(
+            applied_ref[...], rows_ref[...], NT, preferred_element_type=jnp.float32
+        )
+
+    def product(a, b):
+        return lax.dot_general(a, b, NT, preferred_element_type=jnp.float32)
+
+    @pl.when(me < slabs - 1)
+    def _():
+        downward.wait_recv()
+
+    @pl.when(me == slabs - 1)
+    def _():
+        after_ref[...] = jnp.zeros(after_ref.shape, jnp.bfloat16)
+
+    @pl.when(me > 0)
+    def _():
+        upward.wait_recv()
+
+    @pl.when(me == 0)
+    def _():
+        before_ref[...] = jnp.zeros(before_ref.shape, jnp.bfloat16)
+
+    for one in faces:
+        one.wait_recv()
+    weight = -0.5 / PLANE
+
+    @pl.loop(0, 2)
+    def _(index):
+        here = pl.ds(pl.multiple_of(index * block, block), block)
+        joined = product(last_ref[here, :], after_ref[...]) + product(after_ref[here, :], last_ref[...])
+        joined = joined + product(first_ref[here, :], before_ref[...])
+        joined = joined + product(before_ref[here, :], first_ref[...])
+        part_ref[0, here, :] = ((inner_ref[here, :] - joined) * (1.0 / G)).astype(jnp.bfloat16)
+        part_ref[1, here, :] = (product(lz_ref[here, :], rz_in[...]) * weight).astype(jnp.bfloat16)
+        part_ref[2, here, :] = (product(ly_ref[here, :], ry_in[...]) * weight).astype(jnp.bfloat16)
 
     sent = []
     ways = (1, -1)
@@ -386,38 +389,80 @@
         sent += moving
     for ring, way in enumerate(ways):
         hand_on(slabs - 1, ring, way)
-    for one in sent:
+    for one in sent + faces:
         one.wait_send()
+
+    @pl.when(me > 0)
+    def _():
+        downward.wait_send()
+
+    @pl.when(me < slabs - 1)
+    def _():
+        upward.wait_send()
+
     for one in mirrors:
         one.wait()
 
 
-def summed_blocks(partials):
+def summed_blocks(rows, slab_potential, table):
     slabs, elements = lax.axis_size("band"), lax.axis_size("elem")
-    kinds, count, width = partials.shape
+    count, length = rows.shape
     half = count // slabs // 2
+    chunk = face_chunk(length)
+    select = face_selector(chunk)
+    width = length // chunk * (select.shape[1] // 4)
     whole = pl.BlockSpec(memory_space=pltpu.VMEM)
+    dma = pltpu.SemaphoreType.DMA
     return pl.pallas_call(
-        functools.partial(reduce_kernel, slabs, elements),
-        in_specs=[whole],
+        functools.partial(blocks_kernel, slabs, elements),
+        in_specs=[whole] * 4,
         out_specs=[whole, whole],
         out_shape=[
-            jax.ShapeDtypeStruct(partials.shape, jnp.bfloat16),
-            jax.ShapeDtypeStruct((kinds - 1, count, width), jnp.bfloat16),
+            jax.ShapeDtypeStruct((3, count, count), jnp.bfloat16),
+            jax.ShapeDtypeStruct((2, count, count), jnp.bfloat16),
         ],
         scratch_shapes=[
-            pltpu.VMEM((2, slabs - 1, kinds, half, width), jnp.bfloat16),
-            pltpu.SemaphoreType.DMA((2, slabs - 1)),
-            pltpu.SemaphoreType.DMA((2, slabs - 1)),
-            pltpu.SemaphoreType.DMA((2, slabs - 1)),
-            pltpu.SemaphoreType.DMA((2, slabs - 1)),
-            pltpu.SemaphoreType.DMA((2, slabs, kinds - 1)),
-            pltpu.SemaphoreType.DMA((2, slabs, kinds - 1)),
+            pltpu.VMEM((count, padded_width(length)), jnp.bfloat16),
+            pltpu.VMEM((count // 2, length), jnp.bfloat16),
+            pltpu.VMEM((count, count), jnp.float32),
+            pltpu.VMEM((3, count, count), jnp.bfloat16),
+            [pltpu.VMEM((count, PLANE // 2), jnp.bfloat16) for _ in range(6)],
+            [pltpu.VMEM((count, width), jnp.bfloat16) for _ in range(6)],
+            pltpu.VMEM((2, slabs - 1, 3, half, count), jnp.bfloat16),
+            dma((2,)),
+            dma((2,)),
+            dma((2,)),
+            dma((2,)),
+            dma((2, slabs - 1)),
+            dma((2, slabs - 1)),
+            dma((2, slabs - 1)),
+            dma((2, slabs - 1)),
+            dma((2, slabs, 2)),
+            dma((2, slabs, 2)),
         ],
         compiler_params=pltpu.CompilerParams(
             collective_id=0, has_side_effects=True, vmem_limit_bytes=VMEM_LIMIT
         ),
-    )(partials)
+    )(rows, (6.0 + slab_potential)[None], table, select)
+
+
+def apply_blocks(terms, current):
+    offsets = [0, 1, -1, EB, -EB]
+    running = jnp.zeros((terms[0][0].shape[0], current.shape[1]), jnp.float32)
+    for position, offset in enumerate(offsets):
+        matrix, contract = terms[position]
+        if offset == 0:
+            source = current
+        else:
+            source = from_behind(current, "elem", -offset)
+        running = running + lax.dot_general(
+            matrix, source, (((contract,), (0,)), ((), ())), preferred_element_type=jnp.float32
+        )
+    return running
+
+
+def scaled(terms, current):
+    return (apply_blocks(terms, current) - SHIFT_CENTER * current.astype(jnp.float32)) / HALF_WIDTH
 
 
 def on_device(orbitals, potential, basis_count, states):
@@ -433,20 +478,7 @@
     slab_potential = lax.dynamic_slice_in_dim(
         potential[0], band_place * slab_length, slab_length, 0
     )
-    half = PLANE // 2
-    initial, last = basis_rows[:, :PLANE], basis_rows[:, slab_length - PLANE :]
-    up = [(i, i + 1) for i in range(slabs - 1)]
-    down = [(j, i) for i, j in up]
-    after = lax.ppermute(initial[:, :half], "band", down)
-    before = lax.ppermute(last[:, half:], "band", up)
-    lz, rz, ly, ry = face_layers(basis_rows)
-    rz = from_behind(rz, "elem", -1)
-    ry = from_behind(ry, "elem", -EB)
-    inner = interior_block(basis_rows, slab_potential, table)
-    near = jnp.concatenate([last[:, :half], after, initial[:, half:], before], axis=1)
-    far = jnp.concatenate([after, last[:, :half], before, initial[:, half:]], axis=1)
-    partials = partial_blocks(inner, near, far, lz, rz, ly, ry)
-    summed, mirrored = summed_blocks(partials)
+    summed, mirrored = summed_blocks(basis_rows, slab_potential, table)
     terms = [(summed[0], 1), (summed[1], 1), (mirrored[0], 0), (summed[2], 1), (mirrored[1], 0)]
     start_states = states[0]
     first_term = scaled(terms, start_states).astype(jnp.bfloat16)

time: 239 us -> 212 us (0.89)
  local copies, waits for them, and re-layouts: 16.9 us -> 0.01 us
  starting transfers between devices: 22.2 us -> 16.7 us
  matrix products: 8.33 us -> 4.72 us
    unnamed x26 -> x4, local copies, waits for them, and re-layouts: 9.45 us -> 0.01 us
    concatenate x2 -> x0, local copies, waits for them, and re-layouts: 6.07 us -> none  [the longest x1 3.12 us: on_device(): jnp.concatenate([after, last[:, :half], before, initial[:, half:]], axis=1)]
    ppermute x11 -> x9, waiting for transfers between devices: 4.78 us -> 9.14 us  [from_behind(): lax.ppermute(value, axis, [(i, (i + by) % devices) for i in range(devices)])]
    pallas_call x4 -> x1, Pallas kernels: 85.9 us -> 82.3 us  [summed_blocks(): pl.pallas_call(functools.partial(blocks_kernel, slabs, elements), in_spec...]
    dot_general x15, matrix products: 8.33 us -> 4.72 us  [apply_blocks(): lax.dot_general(matrix, source, (((contract,), (0,)), ((), ())), preferre...]
    ppermute x2 -> x0, starting transfers between devices: 3.31 us -> none  [the longest x1 2.03 us: on_device(): before = lax.ppermute(last[:, half:], 'band', up)]
    all_to_all x1, waiting for transfers between devices: 79.1 us -> 76.2 us  [on_device(): lax.all_to_all(basis, 'band', split_axis=0, concat_axis=0, tiled=True)]
    ppermute x11 -> x9, starting transfers between devices: 12.6 us -> 10.2 us  [from_behind(): lax.ppermute(value, axis, [(i, (i + by) % devices) for i in range(devices)])]
  transfers between devices with their start and end apart: 14 -> 10, of which waited for: 4 -> 5; matrix products, arithmetic and copies ran while one was open for 6% -> 2% of each run, Pallas kernels for 36% -> 39%
where the time goes in v4:
time: 212 us
  Pallas kernels  102 us (48%)
  waiting for transfers between devices  85.4 us (40%)
  starting transfers between devices  16.7 us (8%)
  matrix products  4.72 us (2%)
  other arithmetic  2.39 us (1%)
    pallas_call x1, Pallas kernels, summed_blocks(): pl.pallas_call(functools.partial(blocks_kernel, slabs, elements), in_spec...  82.3 us
    all_to_all x1, waiting for transfers between devices, on_device(): lax.all_to_all(basis, 'band', split_axis=0, concat_axis=0, tiled=True)  76.2 us
    pallas_call x1, Pallas kernels, filtered_basis(): pl.pallas_call(functools.partial(filter_kernel, slabs), in_specs=[pl.Bloc...  19.5 us
    ppermute x9, starting transfers between devices, from_behind(): lax.ppermute(value, axis, [(i, (i + by) % devices) for i in range(devices)])  10.2 us
    ppermute x9, waiting for transfers between devices, from_behind(): lax.ppermute(value, axis, [(i, (i + by) % devices) for i in range(devices)])  9.14 us
    all_to_all x1, starting transfers between devices, on_device(): lax.all_to_all(basis, 'band', split_axis=0, concat_axis=0, tiled=True)  6.45 us
    dot_general x15, matrix products, apply_blocks(): lax.dot_general(matrix, source, (((contract,), (0,)), ((), ())), preferre...  4.72 us
  transfers between devices with their start and end apart: 10, of which 5 were waited for; matrix products, arithmetic and copies ran while one was open for 2% of the time, Pallas kernels for 39%

profile of v4, /device:TPU:0, one launch (start us, length us, event | category | flops | bytes accessed | tf_op | source)
XLA Modules:
  0.0 211.7 jit_solution(10586786204993733509)
XLA Ops:
  0.7 0.9 add_multiply_fusion.diag_ref
  1.5 0.1 pad_add_fusion.bounds_ref
  1.6 19.5 %shard_map.64 = bf16[4,128,3456]{2,1,0:T(8,128)(2,1)} custom-call(s32[2]{0:T(128)S(1)} %pad_add_fusion.bounds_ref, bf16[128,13824]{1,0:T(8,128)(2,1)} %bitcast.61, f32[1,13824]{1,0:T(1,128)S(1)} %add_multiply_fusion.diag_ref, bf16[9,1280,256]{2,1,0:T(8,128)(2,1)} %constant.42.clone.table_ref), custom_call_target="tpu_custom_call" | custom-call | tf_op jit(solution)/shard_map/pallas_call | solution.py:129
  21.1 0.0 copy-start.1
  21.1 0.0 copy-start
  21.1 6.5 %all-to-all-start = ((bf16[4,128,3456]{2,1,0:T(8,128)(2,1)}), bf16[4,128,3456]{2,1,0:T(8,128)(2,1)}, u32[]{:S(2)}, u32[]{:S(2)}) async-start(bf16[4,128,3456]{2,1,0:T(8,128)(2,1)} %shard_map.64), calls=%async_computation | async-start | bytes 7077888 | tf_op jit(solution)/shard_map/all_to_all | solution.py:475
  27.6 0.0 copy-done.1
  27.6 1.8 collective-permute-start
  29.4 0.5 collective-permute-start.2
  29.9 0.0 collective-permute-start.1
  29.9 0.7 dynamic-slice_add_fusion.diag_ref
  30.6 76.2 %all-to-all-done = bf16[4,128,3456]{2,1,0:T(8,128)(2,1)} async-done(((bf16[4,128,3456]{2,1,0:T(8,128)(2,1)}), bf16[4,128,3456]{2,1,0:T(8,128)(2,1)}, u32[]{:S(2)}, u32[]{:S(2)}) %all-to-all-start) | async-done | bytes 3538976 | tf_op jit(solution)/shard_map/all_to_all | solution.py:475
  106.8 0.0 copy-done
  106.8 82.3 %shard_map.65 = (bf16[3,512,512]{2,1,0:T(8,128)(2,1)S(1)}, bf16[2,512,512]{2,1,0:T(8,128)(2,1)S(1)}) custom-call(bf16[512,3456]{1,0:T(8,128)(2,1)} %bitcast.2.rows_ref, f32[1,3456]{1,0:T(1,128)S(1)} %dynamic-slice_add_fusion.diag_ref, bf16[9,1280,256]{2,1,0:T(8,128)(2,1)} %constant.42.clone.table_ref, bf16[1152,512]{1,0:T(8,128)(2,1)S(1)} %copy-done), custom_call_target="tpu_custom_call" | custom-call | tf_op jit(solution)/shard_map/pallas_call | solution.py:416
  189.1 0.3 fusion.38
  189.4 0.0 collective-permute-done.2
  189.4 0.3 fusion.26
  189.7 0.0 collective-permute-done
  189.7 0.3 convolution_add_fusion.5
  190.0 0.3 fusion.20
  190.4 0.0 collective-permute-done.1
  190.4 0.4 fusion.15
  190.7 2.9 %collective-permute-start.3 = (bf16[512,128]{1,0:T(8,128)(2,1)S(1)}, bf16[512,128]{1,0:T(8,128)(2,1)S(1)}, u32[]{:S(2)}, u32[]{:S(2)}) collective-permute-start(bf16[512,128]{1,0:T(8,128)(2,1)S(1)} %fusion.15), channel_id=1, source_target_pairs={{0,28},{4,0},{8,4},{12,8},{16,12},{20,16},{24,20},{28,24},{1,29},{... | collective-permute-start | bytes 393224 | tf_op jit(solution)/shard_map/ppermute | solution.py:32
  193.6 1.9 collective-permute-start.5
  195.6 0.0 collective-permute-start.4
  195.6 0.3 fusion.36
  195.9 2.7 %collective-permute-done.5 = bf16[512,128]{1,0:T(8,128)(2,1)S(1)} collective-permute-done((bf16[512,128]{1,0:T(8,128)(2,1)S(1)}, bf16[512,128]{1,0:T(8,128)(2,1)S(1)}, u32[]{:S(2)}, u32[]{:S(2)}) %collective-permute-start.5) | collective-permute-done | bytes 131104 | tf_op jit(solution)/shard_map/ppermute | solution.py:32
  198.6 0.3 fusion.24
  198.9 0.0 collective-permute-done.3
  198.9 0.3 convolution_add_fusion.3
  199.2 0.3 fusion.18
  199.6 2.3 %collective-permute-done.4 = bf16[512,128]{1,0:T(8,128)(2,1)S(1)} collective-permute-done((bf16[512,128]{1,0:T(8,128)(2,1)S(1)}, bf16[512,128]{1,0:T(8,128)(2,1)S(1)}, u32[]{:S(2)}, u32[]{:S(2)}) %collective-permute-start.4) | collective-permute-done | bytes 131104 | tf_op jit(solution)/shard_map/ppermute | solution.py:32
  201.9 0.4 fusion.14
  202.3 1.9 collective-permute-start.6
  204.1 1.2 collective-permute-start.8
  205.3 0.0 collective-permute-start.7
  205.3 0.3 fusion.34
  205.6 3.5 %collective-permute-done.8 = bf16[512,128]{1,0:T(8,128)(2,1)S(1)} collective-permute-done((bf16[512,128]{1,0:T(8,128)(2,1)S(1)}, bf16[512,128]{1,0:T(8,128)(2,1)S(1)}, u32[]{:S(2)}, u32[]{:S(2)}) %collective-permute-start.8) | collective-permute-done | bytes 131104 | tf_op jit(solution)/shard_map/ppermute | solution.py:32
  209.1 0.3 fusion.22
  209.4 0.0 collective-permute-done.6
  209.4 0.3 convolution_add_fusion.1
  209.7 0.3 fusion.16
  210.0 0.6 collective-permute-done.7
  210.6 0.4 multiply_reduce_fusion
  211.0 0.7 fusion.55
  (1 shorter events, 0.0 us)
Async XLA Ops:
  21.1 6.5 %copy-start.1 = (bf16[1,512,128]{2,1,0:T(8,128)(2,1)S(1)}, bf16[1,512,128]{2,1,0:T(8,128)(2,1)}, u32[]{:S(2)}) copy-start(bf16[1,512,128]{2,1,0:T(8,128)(2,1)} %param.9) | copy-start | bytes 393220
  21.1 85.7 %copy-start = (bf16[1152,512]{1,0:T(8,128)(2,1)S(1)}, bf16[1152,512]{1,0:T(8,128)(2,1)}, u32[]{:S(2)}) copy-start(bf16[1152,512]{1,0:T(8,128)(2,1)} %constant.43.clone.select_ref) | copy-start | bytes 3538948
  21.1 85.7 %all-to-all-start = ((bf16[4,128,3456]{2,1,0:T(8,128)(2,1)}), bf16[4,128,3456]{2,1,0:T(8,128)(2,1)}, u32[]{:S(2)}, u32[]{:S(2)}) async-start(bf16[4,128,3456]{2,1,0:T(8,128)(2,1)} %shard_map.64), calls=%async_computation | async-start | bytes 7077888 | tf_op jit(solution)/shard_map/all_to_all | solution.py:475
  27.6 162.1 %collective-permute-start = (bf16[512,128]{1,0:T(8,128)(2,1)S(1)}, bf16[512,128]{1,0:T(8,128)(2,1)S(1)}, u32[]{:S(2)}, u32[]{:S(2)}) collective-permute-start(bf16[512,128]{1,0:T(8,128)(2,1)S(1)} %bitcast.62), channel_id=1, source_target_pairs={{0,28},{4,0},{8,4},{12,8},{16,12},{20,16},{24,20},{28,24},{1,29},{... | collective-permute-start | bytes 393224 | tf_op jit(solution)/shard_map/ppermute | solution.py:32
  29.4 160.0 %collective-permute-start.2 = (bf16[512,128]{1,0:T(8,128)(2,1)S(1)}, bf16[512,128]{1,0:T(8,128)(2,1)S(1)}, u32[]{:S(2)}, u32[]{:S(2)}) collective-permute-start(bf16[512,128]{1,0:T(8,128)(2,1)S(1)} %bitcast.63), channel_id=1, source_target_pairs={{0,16},{4,20},{8,24},{12,28},{16,0},{20,4},{24,8},{28,12},{1,17},{... | collective-permute-start | bytes 393224 | tf_op jit(solution)/shard_map/ppermute | solution.py:32
  29.9 160.5 %collective-permute-start.1 = (bf16[512,128]{1,0:T(8,128)(2,1)S(1)}, bf16[512,128]{1,0:T(8,128)(2,1)S(1)}, u32[]{:S(2)}, u32[]{:S(2)}) collective-permute-start(bf16[512,128]{1,0:T(8,128)(2,1)S(1)} %bitcast.64), channel_id=1, source_target_pairs={{0,4},{4,8},{8,12},{12,16},{16,20},{20,24},{24,28},{28,0},{1,5},{5... | collective-permute-start | bytes 393224 | tf_op jit(solution)/shard_map/ppermute | solution.py:32
  190.7 8.2 %collective-permute-start.3 = (bf16[512,128]{1,0:T(8,128)(2,1)S(1)}, bf16[512,128]{1,0:T(8,128)(2,1)S(1)}, u32[]{:S(2)}, u32[]{:S(2)}) collective-permute-start(bf16[512,128]{1,0:T(8,128)(2,1)S(1)} %fusion.15), channel_id=1, source_target_pairs={{0,28},{4,0},{8,4},{12,8},{16,12},{20,16},{24,20},{28,24},{1,29},{... | collective-permute-start | bytes 393224 | tf_op jit(solution)/shard_map/ppermute | solution.py:32
  193.6 5.0 %collective-permute-start.5 = (bf16[512,128]{1,0:T(8,128)(2,1)S(1)}, bf16[512,128]{1,0:T(8,128)(2,1)S(1)}, u32[]{:S(2)}, u32[]{:S(2)}) collective-permute-start(bf16[512,128]{1,0:T(8,128)(2,1)S(1)} %fusion.15), channel_id=1, source_target_pairs={{0,16},{4,20},{8,24},{12,28},{16,0},{20,4},{24,8},{28,12},{1,17},{... | collective-permute-start | bytes 393224 | tf_op jit(solution)/shard_map/ppermute | solution.py:32
  195.6 6.3 %collective-permute-start.4 = (bf16[512,128]{1,0:T(8,128)(2,1)S(1)}, bf16[512,128]{1,0:T(8,128)(2,1)S(1)}, u32[]{:S(2)}, u32[]{:S(2)}) collective-permute-start(bf16[512,128]{1,0:T(8,128)(2,1)S(1)} %fusion.15), channel_id=1, source_target_pairs={{0,4},{4,8},{8,12},{12,16},{16,20},{20,24},{24,28},{28,0},{1,5},{5... | collective-permute-start | bytes 393224 | tf_op jit(solution)/shard_map/ppermute | solution.py:32
  202.3 7.1 %collective-permute-start.6 = (bf16[512,128]{1,0:T(8,128)(2,1)S(1)}, bf16[512,128]{1,0:T(8,128)(2,1)S(1)}, u32[]{:S(2)}, u32[]{:S(2)}) collective-permute-start(bf16[512,128]{1,0:T(8,128)(2,1)S(1)} %fusion.14), channel_id=1, source_target_pairs={{0,28},{4,0},{8,4},{12,8},{16,12},{20,16},{24,20},{28,24},{1,29},{... | collective-permute-start | bytes 393224 | tf_op jit(solution)/shard_map/ppermute | solution.py:32
  204.1 5.0 %collective-permute-start.8 = (bf16[512,128]{1,0:T(8,128)(2,1)S(1)}, bf16[512,128]{1,0:T(8,128)(2,1)S(1)}, u32[]{:S(2)}, u32[]{:S(2)}) collective-permute-start(bf16[512,128]{1,0:T(8,128)(2,1)S(1)} %fusion.14), channel_id=1, source_target_pairs={{0,16},{4,20},{8,24},{12,28},{16,0},{20,4},{24,8},{28,12},{1,17},{... | collective-permute-start | bytes 393224 | tf_op jit(solution)/shard_map/ppermute | solution.py:32
  205.3 5.3 %collective-permute-start.7 = (bf16[512,128]{1,0:T(8,128)(2,1)S(1)}, bf16[512,128]{1,0:T(8,128)(2,1)S(1)}, u32[]{:S(2)}, u32[]{:S(2)}) collective-permute-start(bf16[512,128]{1,0:T(8,128)(2,1)S(1)} %fusion.14), channel_id=1, source_target_pairs={{0,4},{4,8},{8,12},{12,16},{16,20},{20,24},{24,28},{28,0},{1,5},{5... | collective-permute-start | bytes 393224 | tf_op jit(solution)/shard_map/ppermute | solution.py:32
